TPU v7x, 32 devices: a whole 2x2x4 slice. The times are simulated.
32 devices in a mesh: groups: 2 (over y), expert: 4 (over z), hidden: 4 (over x, core).
Axes of the slice: x: 2, y: 2, z: 4, core: 2. Of those that a mesh axis runs over, the one named last changes fastest.
Arguments:
- tokens: bfloat16 [256, 3072], P(('groups', 'expert'), 'hidden'), parts along dimension 0, may hold values from -6 to 6
- router_weight: float32 [3072, 4], P('hidden'), may hold values from -0.109375 to 0.109375
- routes: int32 [256, 2], P(('groups', 'expert')), parts along dimension 0, may hold values from 0 to 3, as said below
- slots: int32 [256, 2], P(('groups', 'expert')), parts along dimension 0, may hold values from 0 to 127, as said below
- gate_weight: bfloat16 [4, 3072, 16384], P('expert', None, 'hidden'), may hold values from -0.109375 to 0.109375
- up_weight: bfloat16 [4, 3072, 16384], P('expert', None, 'hidden'), may hold values from -0.109375 to 0.109375
- down_weight: bfloat16 [4, 16384, 3072], P('expert', 'hidden'), may hold values from -0.0625 to 0.0625
- scale_exponents: int32 [8, 4, 128, 24], P(('groups', 'expert'), 'hidden'), parts along dimension 0, may hold values from 10 to 13
Outputs:
- mixed: bfloat16 [256, 3072], P(('groups', 'expert'), 'hidden'), parts along dimension 0
There are 2 independent parts, one for each index of `groups`. A program takes and returns all parts, laid end to end along the dimension named above; an argument that names none is the same for every part. Nothing has to cross between parts.
Inputs may be any that keep to these rules, and one draw needn't show every extreme that they name: `routes`: each token names two different experts. For each expert the slots of the tokens routed to it are distinct; the tokens of rows i * 32 to (i + 1) * 32 - 1 have slots from i * 32 to (i + 1) * 32 - 1.
All inputs are finite; a program needn't handle non-finite values.
Results may differ from a plain program's by a relative error of at most 0.01.
Values may be sent and summed in bfloat16 or wider, within the bound.
No kernel may reach another device: no remote copies, remote signals or barrier semaphores. Data moves between devices by JAX's collectives and lax.ppermute only.
A program may use at most 192 MiB of HBM per device.

v0:
```python
import jax
import jax.numpy as jnp
from jax import lax
from jax.sharding import PartitionSpec as P

EXPERTS = 4


def on_device(
    tokens, router_weight, routes, slots, gate_weight, up_weight, down_weight, scale_exponents
):
    slot_count = tokens.shape[0]
    width_dev = tokens.shape[1]
    group = lax.axis_size("expert") // EXPERTS
    source = lax.axis_index("expert")
    partial_logits = jnp.dot(
        tokens.astype(jnp.float32), router_weight, precision=lax.Precision.HIGHEST
    )
    logits = lax.psum(partial_logits, "hidden")
    expert_ids = jnp.arange(EXPERTS, dtype=jnp.int32)
    picked = (routes[:, :, None] == expert_ids[None, None, :]).astype(jnp.float32)
    chosen = jnp.sum(picked * logits[:, None, :], axis=2)
    first_w = jax.nn.sigmoid(chosen[:, 0] - chosen[:, 1])
    second_w = jax.nn.sigmoid(chosen[:, 1] - chosen[:, 0])
    route_w = jnp.stack([first_w, second_w], axis=1)
    local = slots - source * slot_count
    positions = jnp.arange(slot_count, dtype=jnp.int32)
    placed = (local[:, :, None] == positions[None, None, :]).astype(jnp.float32)
    select = jnp.einsum("tke,tks->est", picked, placed).astype(jnp.bfloat16)
    weighted = jnp.einsum("tke,tks,tk->est", picked, placed, route_w)
    gate_w = gate_weight[0]
    up_w = up_weight[0]
    whole = lax.all_gather(tokens, "hidden", axis=1, tiled=True)
    outgoing = jnp.einsum("est,td->esd", select, whole, preferred_element_type=jnp.float32).astype(
        jnp.bfloat16
    )
    outgoing = jnp.repeat(outgoing, group, axis=0)
    arrived = lax.all_to_all(outgoing, "expert", split_axis=0, concat_axis=0, tiled=True)
    rows_in = arrived.reshape(-1, arrived.shape[2])
    gate = jnp.dot(rows_in, gate_w, preferred_element_type=jnp.float32)
    up_val = jnp.dot(rows_in, up_w, preferred_element_type=jnp.float32)
    hidden = (jax.nn.silu(gate) * up_val).astype(jnp.bfloat16)
    partial_value = jnp.dot(hidden, down_weight[0], preferred_element_type=jnp.float32)
    capacity = partial_value.shape[0]
    features = partial_value.shape[1]
    limit = 448.0 * jnp.exp2(-scale_exponents[0, 0].astype(jnp.float32))[:, :, None]
    coded = jnp.clip(partial_value.reshape(capacity, features // 128, 128), -limit, limit).astype(
        jnp.bfloat16
    )
    coded = coded.reshape(capacity, features)
    summed = lax.psum_scatter(
        coded.astype(jnp.float32).astype(jnp.bfloat16), "hidden", scatter_dimension=1, tiled=True
    )
    quarter_out = summed.reshape(-1, slot_count, width_dev)
    returned = lax.all_to_all(quarter_out, "expert", split_axis=0, concat_axis=0, tiled=True)
    expert_out = jnp.sum(
        returned.astype(jnp.float32).reshape(EXPERTS, group, slot_count, width_dev), axis=1
    )
    mixed = jnp.einsum("est,esd->td", weighted, expert_out, precision=lax.Precision.HIGHEST)
    return mixed.astype(jnp.bfloat16)


def solution(mesh):
    placed = (
        P(("groups", "expert"), "hidden"),
        P("hidden", None),
        P(("groups", "expert"), None),
        P(("groups", "expert"), None),
        P("expert", None, "hidden"),
        P("expert", None, "hidden"),
        P("expert", "hidden", None),
        P(("groups", "expert"), "hidden", None, None),
    )
    return jax.shard_map(
        on_device,
        mesh=mesh,
        in_specs=placed,
        out_specs=P(("groups", "expert"), "hidden"),
        check_vma=False,
    )
```

profile of v0, /device:TPU:0, one launch (start us, length us, event | category | flops | bytes accessed | tf_op | source)
XLA Modules:
  0.0 134.2 jit_solution(12359867686283034057)
XLA Ops:
  6.5 0.7 broadcast_subtract_fusion
  7.2 0.1 copy.20
  7.3 0.7 iota_compare_fusion.3
  8.0 0.1 copy.22
  8.1 7.0 %all_gather.3 = bf16[32,3072]{1,0:T(8,128)(2,1)S(1)} all-gather(bf16[32,768]{1,0:T(8,128)(2,1)} %param.8), channel_id=1, replica_groups=mesh['groups'=2,'expert'=4,'hidden'=4] {'hidden'}, dimensions={1}, use_global_device_ids=true | all-gather | bytes 245760 | tf_op jit(solution)/shard_map/all_gather | solution.py:33
  15.2 0.3 fusion.14
  15.5 1.3 convolution_convert_fusion
  16.8 5.1 %all-to-all-start = ((bf16[4,32,3072]{2,1,0:T(8,128)(2,1)}), bf16[4,32,3072]{2,1,0:T(8,128)(2,1)S(1)}, u32[]{:S(2)}, u32[]{:S(2)}) async-start(bf16[4,32,3072]{2,1,0:T(8,128)(2,1)} %convolution_convert_fusion), calls=%async_computation | async-start | bytes 1572864 | tf_op jit(solution)/shard_map/all_to_all | solution.py:38
  21.9 30.8 %copy.28 = bf16[3072,4096]{1,0:T(8,128)(2,1)} copy(bf16[3072,4096]{0,1:T(8,128)(2,1)} %bitcast.46) | data formatting | bytes 50331648 | tf_op jit(solution)/shard_map/dot_general | solution.py:43
  52.7 10.0 %fusion.2 = f32[128,4096]{1,0:T(8,128)S(1)} fusion(bf16[128,3072]{1,0:T(8,128)(2,1)S(1)} %bitcast.47, bf16[1,3072,4096]{2,1,0:T(8,128)(2,1)} %param.12), kind=kOutput, calls=%fused_computation.2 | convolution fusion | flops 3221225472 | bytes 28049408 | tf_op jit(solution)/shard_map/dot_general | solution.py:40
  62.8 12.1 %fusion.10 = bf16[128,4096,1]{1,0,2:T(8,128)(2,1)S(1)} fusion(bf16[128,3072]{1,0:T(8,128)(2,1)S(1)} %bitcast.48, bf16[1,3072,4096]{2,1,0:T(8,128)(2,1)} %param.13, f32[128,4096]{1,0:T(8,128)S(1)} %fusion.2), kind=kOutput, calls=%fused_computation.6 | convolution fusion | flops 3224371200 | bytes 29097984 | tf_op jit(solution)/shard_map/dot_general | solution.py:41
  74.9 0.0 copy-start.1
  74.9 0.0 copy-start.3
  75.0 12.7 %minimum_convert_fusion = bf16[128,24,128]{0,2,1:T(8,128)(2,1)} fusion(bf16[128,4096,1]{1,0,2:T(8,128)(2,1)S(1)} %fusion.10, bf16[24,128,4096]{2,1,0:T(8,128)(2,1)} %bitcast.45, bf16[128,24]{0,1:T(8,128)(2,1)S(1)} %fusion.24, bf16[128,24]{0,1:T(8,128)(2,1)S(1)} %multiply_bitcast_fusion), kind=kOutput, calls=%fused_computation.8 | convolution fusion | flops 3223191552 | bytes 27013120 | tf_op jit(solution)/shard_map/dot_general | solution.py:43
  87.7 0.0 reduce-scatter.2.cloned.1.call-update
  87.7 0.1 fusion.25
  87.8 6.9 %psum.7 = f32[32,4]{0,1:T(4,128)S(1)} all-reduce(f32[32,4]{0,1:T(4,128)S(1)} %fusion.25), channel_id=1, replica_groups=mesh['groups'=2,'expert'=4,'hidden'=4] {'hidden'}, use_global_device_ids=true, to_apply=%region_0.0 | all-reduce | flops 128 | bytes 1024 | tf_op jit(solution)/shard_map/psum | solution.py:19
  94.8 17.8 %reduce-scatter.2.cloned.1.call-done = bf16[128,768]{0,1:T(8,128)(2,1)} async-done(((bf16[128,3072]{0,1:T(8,128)(2,1)}), bf16[128,768]{0,1:T(8,128)(2,1)}) %reduce-scatter.2.cloned.1.call-update) | async-done | bytes 196624 | tf_op jit(solution)/shard_map/reduce_scatter | solution.py:51
  112.6 1.7 %copy.26 = bf16[128,768]{1,0:T(8,128)(2,1)} copy(bf16[128,768]{0,1:T(8,128)(2,1)} %reduce-scatter.2.cloned.1.call-done) | data formatting | bytes 393216 | tf_op jit(solution)/shard_map/reduce_scatter | solution.py:51
  114.3 4.6 %all-to-all-start.1 = ((bf16[4,32,768]{2,1,0:T(8,128)(2,1)}), bf16[4,32,768]{2,1,0:T(8,128)(2,1)S(1)}, u32[]{:S(2)}, u32[]{:S(2)}) async-start(bf16[4,32,768]{2,1,0:T(8,128)(2,1)} %bitcast.12), calls=%async_computation.2 | async-start | bytes 393216 | tf_op jit(solution)/shard_map/all_to_all | solution.py:55
  118.9 0.1 copy.21
  119.0 0.3 convolution_bitcast_fusion.1
  119.3 7.1 %all-to-all-done.1 = bf16[4,32,768]{2,1,0:T(8,128)(2,1)S(1)} async-done(((bf16[4,32,768]{2,1,0:T(8,128)(2,1)}), bf16[4,32,768]{2,1,0:T(8,128)(2,1)S(1)}, u32[]{:S(2)}, u32[]{:S(2)}) %all-to-all-start.1) | async-done | bytes 196640 | tf_op jit(solution)/shard_map/all_to_all | solution.py:55
  126.4 1.0 fusion.13
  (13 shorter events, 0.1 us)
Async XLA Ops:
  6.5 81.2 %copy-start = (f32[768,4]{0,1:T(4,128)S(1)}, f32[768,4]{0,1:T(4,128)}, u32[]{:S(2)}) copy-start(f32[768,4]{0,1:T(4,128)} %param.9) | copy-start | bytes 36868
  16.8 35.9 %all-to-all-start = ((bf16[4,32,3072]{2,1,0:T(8,128)(2,1)}), bf16[4,32,3072]{2,1,0:T(8,128)(2,1)S(1)}, u32[]{:S(2)}, u32[]{:S(2)}) async-start(bf16[4,32,3072]{2,1,0:T(8,128)(2,1)} %convolution_convert_fusion), calls=%async_computation | async-start | bytes 1572864 | tf_op jit(solution)/shard_map/all_to_all | solution.py:38
  21.9 90.7 %reduce-scatter.2.cloned.1.call-start = ((), (), s32[]{:S(2)}) async-start(), calls=%async_computation.3 | async-start | bytes 983040 | tf_op jit(solution)/shard_map/reduce_scatter | solution.py:51
  21.9 30.8 %copy-start.2 = (s32[1,1,128,24]{2,3,1,0:T(8,128)S(1)}, s32[1,1,128,24]{2,3,1,0:T(8,128)}, u32[]{:S(2)}) copy-start(s32[1,1,128,24]{2,3,1,0:T(8,128)} %param.15) | copy-start | bytes 36868
  74.9 12.8 %copy-start.1 = (bf16[32,768]{1,0:T(8,128)(2,1)S(1)}, bf16[32,768]{1,0:T(8,128)(2,1)}, u32[]{:S(2)}) copy-start(bf16[32,768]{1,0:T(8,128)(2,1)} %param.8) | copy-start | bytes 147460
  74.9 19.8 %copy-start.3 = (s32[32,2]{0,1:T(2,128)S(1)}, s32[32,2]{0,1:T(2,128)}, u32[]{:S(2)}) copy-start(s32[32,2]{0,1:T(2,128)} %param.10) | copy-start | bytes 772
  114.3 12.1 %all-to-all-start.1 = ((bf16[4,32,768]{2,1,0:T(8,128)(2,1)}), bf16[4,32,768]{2,1,0:T(8,128)(2,1)S(1)}, u32[]{:S(2)}, u32[]{:S(2)}) async-start(bf16[4,32,768]{2,1,0:T(8,128)(2,1)} %bitcast.12), calls=%async_computation.2 | async-start | bytes 393216 | tf_op jit(solution)/shard_map/all_to_all | solution.py:55
Sparse Core Ops, SparseCore 0:
  87.8 24.7 reduce-scatter.1
where the time goes:
time: 135 us; the launch traced here: 134 us
  matrix products  37.9 us (28%)
  local copies, waits for them, and re-layouts  32.9 us (24%)
  waiting for transfers between devices  25 us (19%)
  blocking collectives  13.9 us (10%)
  between operations  13.5 us (10%)
  starting transfers between devices  9.68 us (7%)
  other arithmetic  1.44 us (1%)
    dot_general x1, local copies, waits for them, and re-layouts, on_device(): jnp.dot(hidden, down_weight[0], preferred_element_type=jnp.float32)  30.8 us
    reduce_scatter x1, waiting for transfers between devices, on_device(): lax.psum_scatter(coded.astype(jnp.float32).astype(jnp.bfloat16), 'hidden'...  17.8 us
    dot_general x1, matrix products, on_device(): jnp.dot(hidden, down_weight[0], preferred_element_type=jnp.float32)  12.7 us
    dot_general x1, matrix products, on_device(): up_val = jnp.dot(rows_in, up_w, preferred_element_type=jnp.float32)  12.1 us
    dot_general x1, matrix products, on_device(): gate = jnp.dot(rows_in, gate_w, preferred_element_type=jnp.float32)  10 us
    all_to_all x1, waiting for transfers between devices, on_device(): lax.all_to_all(quarter_out, 'expert', split_axis=0, concat_axis=0, tiled=...  7.11 us
    all_gather x1, blocking collectives, on_device(): whole = lax.all_gather(tokens, 'hidden', axis=1, tiled=True)  7.05 us
    psum x1, blocking collectives, on_device(): logits = lax.psum(partial_logits, 'hidden')  6.88 us
  transfers between devices with their start and end apart: 3, of which 2 were waited for; matrix products, arithmetic and copies ran while one was open for 23% of the time, Pallas kernels for 0%

commit v1 on v0

--- a/solution.py
+++ b/solution.py
@@ -1,9 +1,20 @@
+import functools
+
 import jax
 import jax.numpy as jnp
 from jax import lax
+from jax.experimental import pallas as pl
+from jax.experimental.pallas import tpu as pltpu
 from jax.sharding import PartitionSpec as P
 
 EXPERTS = 4
+LANES = 128
+BF16 = jnp.bfloat16
+F32 = jnp.float32
+MIB = 1 << 20
+JOINT = ("expert", "hidden")
+VMEM = pl.BlockSpec(memory_space=pltpu.VMEM)
+HBM = pl.BlockSpec(memory_space=pltpu.HBM)
 
 
 def on_device(
@@ -60,6 +71,359 @@
     return mixed.astype(jnp.bfloat16)
 
 
+def swap(value, expert_bits, hidden_bits):
+    pairs = [
+        (e * 4 + h, (e ^ expert_bits) * 4 + (h ^ hidden_bits)) for e in range(4) for h in range(4)
+    ]
+    return lax.ppermute(value, JOINT, pairs)
+
+
+def pack_body(tok_ref, rw_ref, routes_ref, slots_ref, out_ref):
+    rows, width = tok_ref.shape
+    base = lax.axis_index("expert") * rows
+    out_ref[:, :width] = tok_ref[...]
+    values = tok_ref[...].astype(F32)
+    lane = lax.broadcasted_iota(jnp.int32, (rows, LANES), 1)
+    diagonal = lax.broadcasted_iota(jnp.int32, (rows, rows), 0) == lax.broadcasted_iota(
+        jnp.int32, (rows, rows), 1
+    )
+    meta = jnp.zeros((rows, LANES), F32)
+    for expert in range(EXPERTS):
+        logit = jnp.sum(values * rw_ref[expert : expert + 1, :], axis=1, keepdims=True)
+        high = logit.astype(BF16).astype(F32)
+        middle = (logit - high).astype(BF16).astype(F32)
+        low = logit - high - middle
+        code = jnp.zeros((1, rows), F32) - 1.0
+        for pick in range(2):
+            here = (slots_ref[pick : pick + 1, :] - base).astype(F32)
+            code = jnp.where(routes_ref[pick : pick + 1, :] == expert, here, code)
+        column = jnp.sum(jnp.where(diagonal, code, 0.0), axis=1, keepdims=True)
+        for place, term in enumerate((column, high, middle, low)):
+            meta = jnp.where(lane == place * EXPERTS + expert, term, meta)
+    out_ref[:, width:] = meta.astype(BF16)
+
+
+def pack(tokens, router_t, routes_t, slots_t):
+    rows, width = tokens.shape
+    return pl.pallas_call(
+        pack_body,
+        in_specs=[VMEM] * 4,
+        out_specs=VMEM,
+        out_shape=jax.ShapeDtypeStruct((rows, width + LANES), BF16),
+        name="pack",
+    )(tokens, router_t, routes_t, slots_t)
+
+
+def join_body(*refs):
+    out_ref = refs[-1]
+    rows = refs[0].shape[0]
+    for index, ref in enumerate(refs[:-1]):
+        out_ref[index * rows : (index + 1) * rows, :] = ref[...]
+
+
+def join(parts):
+    rows, width = parts[0].shape
+    return pl.pallas_call(
+        join_body,
+        in_specs=[VMEM] * len(parts),
+        out_specs=VMEM,
+        out_shape=jax.ShapeDtypeStruct((rows * len(parts), width), BF16),
+        name="join",
+    )(*parts)
+
+
+def place():
+    hidden = lax.axis_index("hidden")
+    return hidden // 2, hidden % 2
+
+
+def fill_left(left, first, second, core, width):
+    left[:, pl.ds(pl.multiple_of(core * width, LANES), width)] = first[:, :width]
+    left[:, pl.ds(pl.multiple_of((1 - core) * width, LANES), width)] = second[:, :width]
+
+
+NEAR_TILE = 512
+NEAR_SLOTS = 4
+
+
+def near_body(own, mate, wg, wu, acc_g, acc_u, left, buf_g, buf_u, sem_g, sem_u):
+    chip, core = place()
+    width = own.shape[1] - LANES
+    depth = 2 * width
+    tiles = wg.shape[2] // NEAR_TILE
+
+    def copies(index):
+        slot = lax.rem(index, NEAR_SLOTS)
+        rows = pl.ds(pl.multiple_of(chip * depth, LANES), depth)
+        columns = pl.ds(pl.multiple_of(index * NEAR_TILE, NEAR_TILE), NEAR_TILE)
+        return (
+            pltpu.make_async_copy(wg.at[0, rows, columns], buf_g.at[slot], sem_g.at[slot]),
+            pltpu.make_async_copy(wu.at[0, rows, columns], buf_u.at[slot], sem_u.at[slot]),
+        )
+
+    for index in range(NEAR_SLOTS):
+        for copy in copies(index):
+            copy.start()
+    fill_left(left, own, mate, core, width)
+
+    @pl.loop(0, tiles)
+    def _(index):
+        slot = lax.rem(index, NEAR_SLOTS)
+        columns = pl.ds(pl.multiple_of(index * NEAR_TILE, NEAR_TILE), NEAR_TILE)
+        copy_g, copy_u = copies(index)
+        copy_g.wait()
+        acc_g[:, columns] = jnp.dot(left[...], buf_g[slot], preferred_element_type=F32)
+        copy_u.wait()
+        acc_u[:, columns] = jnp.dot(left[...], buf_u[slot], preferred_element_type=F32)
+
+        @pl.when(index + NEAR_SLOTS < tiles)
+        def _():
+            for copy in copies(index + NEAR_SLOTS):
+                copy.start()
+
+
+def near(own, mate, wg, wu):
+    rows, width = own.shape
+    depth = 2 * (width - LANES)
+    units = wg.shape[2]
+    acc = pltpu.VMEM((rows, units), F32)
+    tile = pltpu.VMEM((NEAR_SLOTS, depth, NEAR_TILE), BF16)
+    return pl.pallas_call(
+        near_body,
+        in_specs=[VMEM, VMEM, HBM, HBM],
+        out_specs=[VMEM, VMEM],
+        out_shape=[acc, acc],
+        scratch_shapes=[
+            pltpu.VMEM((rows, depth), BF16),
+            tile,
+            tile,
+            pltpu.SemaphoreType.DMA((NEAR_SLOTS,)),
+            pltpu.SemaphoreType.DMA((NEAR_SLOTS,)),
+        ],
+        cost_estimate=pl.CostEstimate(
+            flops=4 * rows * depth * units, bytes_accessed=4 * depth * units, transcendentals=0
+        ),
+        compiler_params=pltpu.CompilerParams(vmem_limit_bytes=48 * MIB),
+        name="near",
+    )(own, mate, wg, wu)
+
+
+FAR_TILE = 512
+FAR_SLOTS = 4
+DOWN_TILE = 384
+DOWN_SLOTS = 4
+
+
+def far_body(
+    own, mate, cross, cross_mate, acc_g, acc_u, expo, wg, wu, wd, send, keep,
+    left, hid, limits, share, buf_g, buf_u, buf_d, sem_g, sem_u, sem_d,
+):
+    chip, core = place()
+    expert = lax.axis_index("expert")
+    rows = own.shape[0]
+    width = own.shape[1] - LANES
+    depth = 2 * width
+    tiles = wg.shape[2] // FAR_TILE
+    parts = width // DOWN_TILE
+    half = 2 * parts
+    down_tiles = 2 * half
+
+    def copies(index):
+        slot = lax.rem(index, FAR_SLOTS)
+        there = pl.ds(pl.multiple_of((1 - chip) * depth, LANES), depth)
+        columns = pl.ds(pl.multiple_of(index * FAR_TILE, FAR_TILE), FAR_TILE)
+        return (
+            pltpu.make_async_copy(wg.at[0, there, columns], buf_g.at[slot], sem_g.at[slot]),
+            pltpu.make_async_copy(wu.at[0, there, columns], buf_u.at[slot], sem_u.at[slot]),
+        )
+
+    def owner(index):
+        block = index // parts
+        to_chip = jnp.where(lax.rem(block, 2) == 0, chip, 1 - chip)
+        to_core = jnp.where(block < 2, 1 - core, core)
+        return 2 * to_chip + to_core
+
+    def down_copy(index):
+        slot = lax.rem(index, DOWN_SLOTS)
+        start = owner(index) * width + lax.rem(index, parts) * DOWN_TILE
+        columns = pl.ds(pl.multiple_of(start, LANES), DOWN_TILE)
+        return pltpu.make_async_copy(wd.at[0, :, columns], buf_d.at[slot], sem_d.at[slot])
+
+    for index in range(FAR_SLOTS):
+        for copy in copies(index):
+            copy.start()
+    fill_left(left, cross, cross_mate, core, width)
+
+    meta = own[:, width:].astype(F32)
+    lane = lax.broadcasted_iota(jnp.int32, meta.shape, 1)
+    terms = meta
+    for ref in (mate, cross, cross_mate):
+        terms = terms + ref[:, width:].astype(F32)
+
+    def column(table, index):
+        return jnp.sum(jnp.where(lane == index, table, 0.0), axis=1, keepdims=True)
+
+    code = column(meta, expert)
+    first = jnp.zeros((rows, 1), F32)
+    other = jnp.zeros((rows, 1), F32)
+    for index in range(EXPERTS):
+        used = (lane >= EXPERTS) & (lane < 4 * EXPERTS) & (lax.rem(lane, EXPERTS) == index)
+        logit = jnp.sum(jnp.where(used, terms, 0.0), axis=1, keepdims=True)
+        routed = meta[:, index : index + 1] >= 0.0
+        first = jnp.where(index == expert, logit, first)
+        other = jnp.where(routed & (index != expert), logit, other)
+    weight = jnp.where(code >= 0.0, 1.0 / (1.0 + jnp.exp(other - first)), 0.0)
+    share[...] = jnp.broadcast_to(weight, share.shape)
+    slots_each = rows // EXPERTS
+    row = lax.broadcasted_iota(jnp.int32, (rows, rows), 0)
+    source = jnp.bitwise_xor(row // slots_each, expert)
+    target = jnp.where(code >= 0.0, (source * slots_each).astype(F32) + code, -1.0)
+    chosen = lax.broadcasted_iota(jnp.int32, (rows, rows), 1).astype(F32) == target
+    table = 448.0 * jnp.exp2(-expo[...].astype(F32))
+    limit = lax.dot_general(
+        chosen.astype(BF16), table.astype(BF16), (((1,), (1,)), ((), ())), preferred_element_type=F32
+    )
+    for index in range(limits.shape[0]):
+        limits[index] = jnp.broadcast_to(limit[:, index : index + 1], (rows, LANES))
+
+    @pl.loop(0, tiles)
+    def _(index):
+        slot = lax.rem(index, FAR_SLOTS)
+        columns = pl.ds(pl.multiple_of(index * FAR_TILE, FAR_TILE), FAR_TILE)
+        copy_g, copy_u = copies(index)
+        copy_g.wait()
+        gate = acc_g[:, columns] + jnp.dot(left[...], buf_g[slot], preferred_element_type=F32)
+        copy_u.wait()
+        up = acc_u[:, columns] + jnp.dot(left[...], buf_u[slot], preferred_element_type=F32)
+        hid[:, columns] = (gate / (1.0 + jnp.exp(-gate)) * up).astype(BF16)
+
+        @pl.when(index + FAR_SLOTS < tiles)
+        def _():
+            for copy in copies(index + FAR_SLOTS):
+                copy.start()
+
+        @pl.when(index + DOWN_SLOTS >= tiles)
+        def _():
+            down_copy(index + DOWN_SLOTS - tiles).start()
+
+    def down(index, out, block):
+        down_copy(index).wait()
+        partial = jnp.dot(hid[...], buf_d[lax.rem(index, DOWN_SLOTS)], preferred_element_type=F32)
+        pieces = []
+        for piece in range(DOWN_TILE // LANES):
+            feature = (owner(index) * width + lax.rem(index, parts) * DOWN_TILE) // LANES + piece
+            bound = limits[feature]
+            value = partial[:, piece * LANES : (piece + 1) * LANES]
+            coded = jnp.clip(value, -bound, bound).astype(BF16).astype(F32)
+            pieces.append(coded * share[...])
+        columns = pl.ds(pl.multiple_of(lax.rem(index, parts) * DOWN_TILE, LANES), DOWN_TILE)
+        out[block, :, columns] = jnp.concatenate(pieces, axis=1).astype(out.dtype)
+
+        @pl.when(index + DOWN_SLOTS < down_tiles)
+        def _():
+            down_copy(index + DOWN_SLOTS).start()
+
+    @pl.loop(0, half)
+    def _(index):
+        down(index, send, index // parts)
+
+    @pl.loop(0, half)
+    def _(index):
+        down(index + half, keep, index // parts)
+
+
+def far(own, mate, cross, cross_mate, acc_g, acc_u, expo, wg, wu, wd):
+    rows, width = own.shape
+    width = width - LANES
+    depth = 2 * width
+    units = wg.shape[2]
+    tile = pltpu.VMEM((FAR_SLOTS, depth, FAR_TILE), BF16)
+    return pl.pallas_call(
+        far_body,
+        in_specs=[VMEM] * 7 + [HBM] * 3,
+        out_specs=[VMEM, VMEM],
+        out_shape=[
+            jax.ShapeDtypeStruct((2, rows, width), BF16),
+            jax.ShapeDtypeStruct((2, rows, width), F32),
+        ],
+        scratch_shapes=[
+            pltpu.VMEM((rows, depth), BF16),
+            pltpu.VMEM((rows, units), BF16),
+            pltpu.VMEM((expo.shape[0], rows, LANES), F32),
+            pltpu.VMEM((rows, LANES), F32),
+            tile,
+            tile,
+            pltpu.VMEM((DOWN_SLOTS, units, DOWN_TILE), BF16),
+            pltpu.SemaphoreType.DMA((FAR_SLOTS,)),
+            pltpu.SemaphoreType.DMA((FAR_SLOTS,)),
+            pltpu.SemaphoreType.DMA((DOWN_SLOTS,)),
+        ],
+        cost_estimate=pl.CostEstimate(
+            flops=8 * rows * depth * units, bytes_accessed=8 * depth * units, transcendentals=0
+        ),
+        compiler_params=pltpu.CompilerParams(vmem_limit_bytes=48 * MIB),
+        name="far",
+    )(own, mate, cross, cross_mate, acc_g, acc_u, expo, wg, wu, wd)
+
+
+def split_body(keep, got, *outs):
+    rows = outs[0].shape[0]
+    for index, out in enumerate(outs):
+        chip, block = index // EXPERTS, index % EXPERTS
+        piece = slice(block * rows, (block + 1) * rows)
+        out[...] = (keep[chip, piece, :] + got[chip, piece, :].astype(F32)).astype(out.dtype)
+
+
+def split(keep, got):
+    rows, width = keep.shape[1] // EXPERTS, keep.shape[2]
+    kinds = [F32] + [BF16] * (2 * EXPERTS - 1)
+    return pl.pallas_call(
+        split_body,
+        in_specs=[VMEM, VMEM],
+        out_specs=[VMEM] * len(kinds),
+        out_shape=[jax.ShapeDtypeStruct((rows, width), kind) for kind in kinds],
+        name="split",
+    )(keep, got)
+
+
+def total_body(*refs):
+    total = refs[0][...]
+    for ref in refs[1:-1]:
+        total = total + ref[...].astype(F32)
+    refs[-1][...] = total.astype(BF16)
+
+
+def total(parts):
+    return pl.pallas_call(
+        total_body,
+        in_specs=[VMEM] * len(parts),
+        out_specs=VMEM,
+        out_shape=jax.ShapeDtypeStruct(parts[0].shape, BF16),
+        name="total",
+    )(*parts)
+
+
+def fast(tokens, router_weight, routes, slots, gate_weight, up_weight, down_weight, scale_exponents):
+    packed = pack(tokens, router_weight.T, routes.T, slots.T)
+    own = join([packed] + [swap(packed, bits, 0) for bits in (1, 2, 3)])
+    mate = swap(own, 0, 1)
+    cross = swap(own, 0, 2)
+    acc_g, acc_u = near(own, mate, gate_weight, up_weight)
+    cross_mate = swap(cross, 0, 1)
+    send, keep = far(
+        own, mate, cross, cross_mate, acc_g, acc_u, scale_exponents[0, 0].T,
+        gate_weight, up_weight, down_weight,
+    )
+    got = swap(send, 0, 1)
+    blocks = split(keep, got)
+    parts = [blocks[0]]
+    for bits in (3, 2, 1):
+        for chip in (2, 0):
+            parts.append(swap(blocks[(chip // 2) * EXPERTS + bits], bits, chip))
+    parts.append(swap(blocks[EXPERTS], 0, 2))
+    return total(parts)
+
+
 def solution(mesh):
     placed = (
         P(("groups", "expert"), "hidden"),
@@ -71,8 +435,9 @@
         P("expert", "hidden", None),
         P(("groups", "expert"), "hidden", None, None),
     )
+    general = mesh.shape["expert"] != 4 or mesh.shape["hidden"] != 4
     return jax.shard_map(
-        on_device,
+        on_device if general else fast,
         mesh=mesh,
         in_specs=placed,
         out_specs=P(("groups", "expert"), "hidden"),

time: 135 us -> 74.8 us (0.55)
  matrix products: 37.9 us -> 0 us
  Pallas kernels: 0 us -> 34.6 us
  local copies, waits for them, and re-layouts: 32.9 us -> 5.75 us
  blocking collectives: 13.9 us -> 0 us
  between operations: 13.5 us -> 0.09 us
  waiting for transfers between devices: 25 us -> 15.3 us
  starting transfers between devices: 9.68 us -> 18.8 us
  other arithmetic: 1.44 us -> 0 us
    dot_general x8 -> x0, matrix products: 37.9 us -> none  [the longest x1 12.7 us: on_device(): jnp.dot(hidden, down_weight[0], preferred_element_type=jnp.float32)]
    pallas_call x0 -> x6, Pallas kernels: none -> 34.6 us  [the longest x1 18.7 us: far(): pl.pallas_call(far_body, in_specs=[VMEM] * 7 + [HBM] * 3, out_specs=[VMEM...]
    dot_general x1 -> x0, local copies, waits for them, and re-layouts: 30.8 us -> none  [on_device(): jnp.dot(hidden, down_weight[0], preferred_element_type=jnp.float32)]
    ppermute x0 -> x14, starting transfers between devices: none -> 18.8 us  [swap(): return lax.ppermute(value, JOINT, pairs)]
    reduce_scatter x1 -> x0, waiting for transfers between devices: 17.8 us -> none  [on_device(): lax.psum_scatter(coded.astype(jnp.float32).astype(jnp.bfloat16), 'hidden'...]
    ppermute x0 -> x14, waiting for transfers between devices: none -> 15.3 us  [swap(): return lax.ppermute(value, JOINT, pairs)]
    all_to_all x2 -> x0, starting transfers between devices: 9.67 us -> none  [the longest x1 5.09 us: on_device(): lax.all_to_all(outgoing, 'expert', split_axis=0, concat_axis=0, tiled=True)]
    all_to_all x2 -> x0, waiting for transfers between devices: 7.11 us -> none  [the longest x1 7.11 us: on_device(): lax.all_to_all(quarter_out, 'expert', split_axis=0, concat_axis=0, tiled=...]
  transfers between devices with their start and end apart: 3 -> 14, of which waited for: 2 -> 9; matrix products, arithmetic and copies ran while one was open for 23% -> 0% of each run, Pallas kernels for 0% -> 12%
where the time goes in v1:
time: 74.8 us; the launch traced here: 74.5 us
  Pallas kernels  34.6 us (46%)
  starting transfers between devices  18.8 us (25%)
  waiting for transfers between devices  15.3 us (20%)
  local copies, waits for them, and re-layouts  5.75 us (8%)
    ppermute x14, starting transfers between devices, swap(): return lax.ppermute(value, JOINT, pairs)  18.8 us
    pallas_call x1, Pallas kernels, far(): pl.pallas_call(far_body, in_specs=[VMEM] * 7 + [HBM] * 3, out_specs=[VMEM...  18.7 us
    ppermute x14, waiting for transfers between devices, swap(): return lax.ppermute(value, JOINT, pairs)  15.3 us
    pallas_call x1, Pallas kernels, near(): pl.pallas_call(near_body, in_specs=[VMEM, VMEM, HBM, HBM], out_specs=[VME...  9.08 us
    unnamed x30, local copies, waits for them, and re-layouts  5.75 us
    pallas_call x1, Pallas kernels, split(): pl.pallas_call(split_body, in_specs=[VMEM, VMEM], out_specs=[VMEM] * len(...  1.99 us
    pallas_call x1, Pallas kernels, total(): pl.pallas_call(total_body, in_specs=[VMEM] * len(parts), out_specs=VMEM,...  1.66 us
    pallas_call x1, Pallas kernels, join(): pl.pallas_call(join_body, in_specs=[VMEM] * len(parts), out_specs=VMEM, o...  1.62 us
  transfers between devices with their start and end apart: 14, of which 9 were waited for; matrix products, arithmetic and copies ran while one was open for 0% of the time, Pallas kernels for 12%

profile of v1, /device:TPU:0, one launch (start us, length us, event | category | flops | bytes accessed | tf_op | source)
XLA Modules:
  0.0 74.5 jit_solution(6051230815376286324)
XLA Ops:
  0.0 1.6 %pack.1.refs_0_ = bf16[32,896]{1,0:T(8,128)(2,1)} custom-call(bf16[32,768]{1,0:T(8,128)(2,1)} %tok_ref.1, f32[4,768]{1,0:T(4,128)} %bitcast.7, s32[2,32]{1,0:T(2,128)} %bitcast.8, s32[2,32]{1,0:T(2,128)} %bitcast.9), custom_call_target="tpu_custom_call" | custom-call | tf_op jit(solution)/shard_map/pack/pallas_call | solution.py:108
  1.6 5.0 %collective-permute-start.2 = (bf16[32,896]{1,0:T(8,128)(2,1)}, bf16[32,896]{1,0:T(8,128)(2,1)S(1)}, u32[]{:S(2)}, u32[]{:S(2)}) collective-permute-start(bf16[32,896]{1,0:T(8,128)(2,1)} %pack.1.refs_0_), channel_id=1, source_target_pairs={{0,12},{1,13},{2,14},{3,15},{4,8},{5,9},{6,10},{7,11},{8,4},{9,5},... | collective-permute-start | bytes 172040 | tf_op jit(solution)/shard_map/ppermute | solution.py:78
  7.2 2.1 %collective-permute-done.2.refs_3_ = bf16[32,896]{1,0:T(8,128)(2,1)S(1)} collective-permute-done((bf16[32,896]{1,0:T(8,128)(2,1)}, bf16[32,896]{1,0:T(8,128)(2,1)S(1)}, u32[]{:S(2)}, u32[]{:S(2)}) %collective-permute-start.2) | collective-permute-done | bytes 57376 | tf_op jit(solution)/shard_map/ppermute | solution.py:78
  9.3 2.6 %collective-permute-done.1.refs_2_ = bf16[32,896]{1,0:T(8,128)(2,1)S(1)} collective-permute-done((bf16[32,896]{1,0:T(8,128)(2,1)}, bf16[32,896]{1,0:T(8,128)(2,1)S(1)}, u32[]{:S(2)}, u32[]{:S(2)}) %collective-permute-start.1) | collective-permute-done | bytes 57376 | tf_op jit(solution)/shard_map/ppermute | solution.py:78
  12.5 0.6 copy-done.7
  13.1 1.6 %join.1.own = bf16[128,896]{1,0:T(8,128)(2,1)} custom-call(bf16[32,896]{1,0:T(8,128)(2,1)} %pack.1.refs_0_, bf16[32,896]{1,0:T(8,128)(2,1)} %copy-done.7, bf16[32,896]{1,0:T(8,128)(2,1)} %copy-done.6, bf16[32,896]{1,0:T(8,128)(2,1)} %copy-done.5), custom_call_target="tpu_custom_call" | custom-call | tf_op jit(solution)/shard_map/join/pallas_call | solution.py:126
  14.8 1.5 %collective-permute-start.4 = (bf16[128,896]{1,0:T(8,128)(2,1)}, bf16[128,896]{1,0:T(8,128)(2,1)S(1)}, u32[]{:S(2)}, u32[]{:S(2)}) collective-permute-start(bf16[128,896]{1,0:T(8,128)(2,1)} %join.1.own), channel_id=1, source_target_pairs={{0,2},{1,3},{2,0},{3,1},{4,6},{5,7},{6,4},{7,5},{8,10},{9,11},{10,... | collective-permute-start | bytes 688136 | tf_op jit(solution)/shard_map/ppermute | solution.py:78
  16.3 5.3 %collective-permute-done.4.cross = bf16[128,896]{1,0:T(8,128)(2,1)S(1)} collective-permute-done((bf16[128,896]{1,0:T(8,128)(2,1)}, bf16[128,896]{1,0:T(8,128)(2,1)S(1)}, u32[]{:S(2)}, u32[]{:S(2)}) %collective-permute-start.4) | collective-permute-done | bytes 229408 | tf_op jit(solution)/shard_map/ppermute | solution.py:78
  21.6 0.9 %copy-done.1 = bf16[128,896]{1,0:T(8,128)(2,1)S(1)} copy-done((bf16[128,896]{1,0:T(8,128)(2,1)S(1)}, bf16[128,896]{1,0:T(8,128)(2,1)}, u32[]{:S(2)}) %copy-start.1) | copy-done | bytes 229400
  22.6 9.1 %near.1 = (f32[128,4096]{1,0:T(8,128)S(1)}, f32[128,4096]{1,0:T(8,128)S(1)}) custom-call(bf16[128,896]{1,0:T(8,128)(2,1)S(1)} %copy-done.1, bf16[128,896]{1,0:T(8,128)(2,1)S(1)} %collective-permute-done.3.mate, bf16[1,3072,4096]{2,1,0:T(8,128)(2,1)} %wg.3, bf16[1,3072,4096]{2,1,0:T(8,128)(2,1)} %wu.3), custom_call_target="tpu_custom_call" | custom-call | flops 3221225472 | bytes 25165824 | tf_op jit(solution)/shard_map/near/pallas_call | solution.py:191
  31.7 1.3 %copy-done = f32[128,4096]{1,0:T(8,128)} copy-done((f32[128,4096]{1,0:T(8,128)}, f32[128,4096]{1,0:T(8,128)S(1)}, u32[]{:S(2)}) %copy-start) | copy-done | bytes 2097176
  33.0 18.7 %far.1 = (bf16[2,128,768]{2,1,0:T(8,128)(2,1)S(1)}, f32[2,128,768]{2,1,0:T(8,128)S(1)}) custom-call(bf16[128,896]{1,0:T(8,128)(2,1)S(1)} %copy-done.1, bf16[128,896]{1,0:T(8,128)(2,1)S(1)} %collective-permute-done.3.mate, bf16[128,896]{1,0:T(8,128)(2,1)S(1)} %collective-permute-done.4.cross, bf16[128,896]{1,0:T(8,128)(2,1)S(1)} %collective-permute-done.5.cross_mate, ...), custom_call_target="tpu_custom_call" | custom-call | flops 6442450944 | bytes 50331648 | tf_op jit(solution)/shard_map/far/pallas_call | solution.py:341
  51.7 0.9 %copy-done.2 = f32[2,128,768]{2,1,0:T(8,128)} copy-done((f32[2,128,768]{2,1,0:T(8,128)}, f32[2,128,768]{2,1,0:T(8,128)S(1)}, u32[]{:S(2)}) %copy-start.2) | copy-done | bytes 786456
  53.1 1.3 %collective-permute-done.6.got = bf16[2,128,768]{2,1,0:T(8,128)(2,1)S(1)} collective-permute-done((bf16[2,128,768]{2,1,0:T(8,128)(2,1)S(1)}, bf16[2,128,768]{2,1,0:T(8,128)(2,1)S(1)}, u32[]{:S(2)}, u32[]{:S(2)}) %collective-permute-start.6) | collective-permute-done | bytes 393248 | tf_op jit(solution)/shard_map/ppermute | solution.py:78
  54.5 0.8 %copy-done.4 = bf16[2,128,768]{2,1,0:T(8,128)(2,1)} copy-done((bf16[2,128,768]{2,1,0:T(8,128)(2,1)}, bf16[2,128,768]{2,1,0:T(8,128)(2,1)S(1)}, u32[]{:S(2)}) %copy-start.4) | copy-done | bytes 393240
  55.2 2.0 %split.1 = (f32[32,768]{1,0:T(8,128)}, bf16[32,768]{1,0:T(8,128)(2,1)}, bf16[32,768]{1,0:T(8,128)(2,1)}, bf16[32,768]{1,0:T(8,128)(2,1)}, bf16[32,768]{1,0:T(8,1...) custom-call(f32[2,128,768]{2,1,0:T(8,128)} %copy-done.2, ...), custom_call_target="tpu_custom_call" | custom-call | tf_op jit(solution)/shard_map/split/pallas_call | solution.py:380
  57.2 2.9 %collective-permute-start.7 = (bf16[32,768]{1,0:T(8,128)(2,1)}, bf16[32,768]{1,0:T(8,128)(2,1)S(1)}, u32[]{:S(2)}, u32[]{:S(2)}) collective-permute-start(bf16[32,768]{1,0:T(8,128)(2,1)} %get-tuple-element.22), channel_id=1, source_target_pairs={{0,14},{1,15},{2,12},{3,13},{4,10},{5,11},{6,8},{7,9},{8,6},{9,7},... | collective-permute-start | bytes 147464 | tf_op jit(solution)/shard_map/ppermute | solution.py:78
  60.1 2.0 %collective-permute-start.8 = (bf16[32,768]{1,0:T(8,128)(2,1)}, bf16[32,768]{1,0:T(8,128)(2,1)S(1)}, u32[]{:S(2)}, u32[]{:S(2)}) collective-permute-start(bf16[32,768]{1,0:T(8,128)(2,1)} %get-tuple-element.23), channel_id=1, source_target_pairs={{0,12},{1,13},{2,14},{3,15},{4,8},{5,9},{6,10},{7,11},{8,4},{9,5},... | collective-permute-start | bytes 147464 | tf_op jit(solution)/shard_map/ppermute | solution.py:78
  62.1 2.8 %collective-permute-start.10 = (bf16[32,768]{1,0:T(8,128)(2,1)}, bf16[32,768]{1,0:T(8,128)(2,1)S(1)}, u32[]{:S(2)}, u32[]{:S(2)}) collective-permute-start(bf16[32,768]{1,0:T(8,128)(2,1)} %get-tuple-element.25), channel_id=1, source_target_pairs={{0,8},{1,9},{2,10},{3,11},{4,12},{5,13},{6,14},{7,15},{8,0},{9,1},... | collective-permute-start | bytes 147464 | tf_op jit(solution)/shard_map/ppermute | solution.py:78
  65.4 2.5 %collective-permute-start.12 = (bf16[32,768]{1,0:T(8,128)(2,1)}, bf16[32,768]{1,0:T(8,128)(2,1)S(1)}, u32[]{:S(2)}, u32[]{:S(2)}) collective-permute-start(bf16[32,768]{1,0:T(8,128)(2,1)} %get-tuple-element.27), channel_id=1, source_target_pairs={{0,4},{1,5},{2,6},{3,7},{4,0},{5,1},{6,2},{7,3},{8,12},{9,13},{10,... | collective-permute-start | bytes 147464 | tf_op jit(solution)/shard_map/ppermute | solution.py:78
  68.4 0.7 collective-permute-done.9.refs_3_
  69.1 1.1 %collective-permute-done.10.refs_4_ = bf16[32,768]{1,0:T(8,128)(2,1)S(1)} collective-permute-done((bf16[32,768]{1,0:T(8,128)(2,1)}, bf16[32,768]{1,0:T(8,128)(2,1)S(1)}, u32[]{:S(2)}, u32[]{:S(2)}) %collective-permute-start.10) | collective-permute-done | bytes 49184 | tf_op jit(solution)/shard_map/ppermute | solution.py:78
  70.5 1.1 %collective-permute-done.12.refs_6_ = bf16[32,768]{1,0:T(8,128)(2,1)S(1)} collective-permute-done((bf16[32,768]{1,0:T(8,128)(2,1)}, bf16[32,768]{1,0:T(8,128)(2,1)S(1)}, u32[]{:S(2)}, u32[]{:S(2)}) %collective-permute-start.12) | collective-permute-done | bytes 49184 | tf_op jit(solution)/shard_map/ppermute | solution.py:78
  72.8 1.7 %total.1 = bf16[32,768]{1,0:T(8,128)(2,1)} custom-call(f32[32,768]{1,0:T(8,128)} %get-tuple-element.21.refs_0_, bf16[32,768]{1,0:T(8,128)(2,1)} %copy-done.8, bf16[32,768]{1,0:T(8,128)(2,1)} %copy-done.9, bf16[32,768]{1,0:T(8,128)(2,1)} %copy-done.10, bf16[32,768]{1,0:T(8,128)(2,1)} %copy-done.11, bf16[32,768]{1,0:T(8,128)(2,1)} %copy-done.12, ...), custom_call_target="tpu_custom_call" | custom-call | tf_op jit(solution)/shard_map/total/pallas_call | solution.py:397
  (40 shorter events, 4.3 us)
Async XLA Ops:
  1.6 7.7 %collective-permute-start.2 = (bf16[32,896]{1,0:T(8,128)(2,1)}, bf16[32,896]{1,0:T(8,128)(2,1)S(1)}, u32[]{:S(2)}, u32[]{:S(2)}) collective-permute-start(bf16[32,896]{1,0:T(8,128)(2,1)} %pack.1.refs_0_), channel_id=1, source_target_pairs={{0,12},{1,13},{2,14},{3,15},{4,8},{5,9},{6,10},{7,11},{8,4},{9,5},... | collective-permute-start | bytes 172040 | tf_op jit(solution)/shard_map/ppermute | solution.py:78
  6.6 5.3 %collective-permute-start.1 = (bf16[32,896]{1,0:T(8,128)(2,1)}, bf16[32,896]{1,0:T(8,128)(2,1)S(1)}, u32[]{:S(2)}, u32[]{:S(2)}) collective-permute-start(bf16[32,896]{1,0:T(8,128)(2,1)} %pack.1.refs_0_), channel_id=1, source_target_pairs={{0,8},{1,9},{2,10},{3,11},{4,12},{5,13},{6,14},{7,15},{8,0},{9,1},... | collective-permute-start | bytes 172040 | tf_op jit(solution)/shard_map/ppermute | solution.py:78
  6.6 5.3 %collective-permute-start = (bf16[32,896]{1,0:T(8,128)(2,1)}, bf16[32,896]{1,0:T(8,128)(2,1)S(1)}, u32[]{:S(2)}, u32[]{:S(2)}) collective-permute-start(bf16[32,896]{1,0:T(8,128)(2,1)} %pack.1.refs_0_), channel_id=1, source_target_pairs={{0,4},{1,5},{2,6},{3,7},{4,0},{5,1},{6,2},{7,3},{8,12},{9,13},{10,... | collective-permute-start | bytes 172040 | tf_op jit(solution)/shard_map/ppermute | solution.py:78
  9.2 2.7 %copy-start.5 = (bf16[32,896]{1,0:T(8,128)(2,1)}, bf16[32,896]{1,0:T(8,128)(2,1)S(1)}, u32[]{:S(2)}) copy-start(bf16[32,896]{1,0:T(8,128)(2,1)S(1)} %collective-permute-done.2.refs_3_) | copy-start | bytes 172036
  13.1 19.9 %copy-start.3 = (s32[1,1,128,24]{2,3,1,0:T(8,128)S(1)}, s32[1,1,128,24]{2,3,1,0:T(8,128)}, u32[]{:S(2)}) copy-start(s32[1,1,128,24]{2,3,1,0:T(8,128)} %param.15) | copy-start | bytes 36868
  14.8 6.8 %collective-permute-start.4 = (bf16[128,896]{1,0:T(8,128)(2,1)}, bf16[128,896]{1,0:T(8,128)(2,1)S(1)}, u32[]{:S(2)}, u32[]{:S(2)}) collective-permute-start(bf16[128,896]{1,0:T(8,128)(2,1)} %join.1.own), channel_id=1, source_target_pairs={{0,2},{1,3},{2,0},{3,1},{4,6},{5,7},{6,4},{7,5},{8,10},{9,11},{10,... | collective-permute-start | bytes 688136 | tf_op jit(solution)/shard_map/ppermute | solution.py:78
  16.3 5.3 %collective-permute-start.3 = (bf16[128,896]{1,0:T(8,128)(2,1)}, bf16[128,896]{1,0:T(8,128)(2,1)S(1)}, u32[]{:S(2)}, u32[]{:S(2)}) collective-permute-start(bf16[128,896]{1,0:T(8,128)(2,1)} %join.1.own), channel_id=1, source_target_pairs={{0,1},{1,0},{2,3},{3,2},{4,5},{5,4},{6,7},{7,6},{8,9},{9,8},{10,11... | collective-permute-start | bytes 688136 | tf_op jit(solution)/shard_map/ppermute | solution.py:78
  21.6 11.4 %collective-permute-start.5 = (bf16[128,896]{1,0:T(8,128)(2,1)S(1)}, bf16[128,896]{1,0:T(8,128)(2,1)S(1)}, u32[]{:S(2)}, u32[]{:S(2)}) collective-permute-start(bf16[128,896]{1,0:T(8,128)(2,1)S(1)} %collective-permute-done.4.cross), channel_id=1, source_target_pairs={{0,1},{1,0},{2,3},{3,2},{4,5},{5,4},{6,7},{7,6},{8,9},{9,8},{10,11... | collective-permute-start | bytes 688136 | tf_op jit(solution)/shard_map/ppermute | solution.py:78
  21.6 0.9 %copy-start.1 = (bf16[128,896]{1,0:T(8,128)(2,1)S(1)}, bf16[128,896]{1,0:T(8,128)(2,1)}, u32[]{:S(2)}) copy-start(bf16[128,896]{1,0:T(8,128)(2,1)} %join.1.own) | copy-start | bytes 688132
  31.6 1.3 %copy-start = (f32[128,4096]{1,0:T(8,128)}, f32[128,4096]{1,0:T(8,128)S(1)}, u32[]{:S(2)}) copy-start(f32[128,4096]{1,0:T(8,128)S(1)} %get-tuple-element.18.acc_u) | copy-start | bytes 6291460
  51.7 0.9 %copy-start.2 = (f32[2,128,768]{2,1,0:T(8,128)}, f32[2,128,768]{2,1,0:T(8,128)S(1)}, u32[]{:S(2)}) copy-start(f32[2,128,768]{2,1,0:T(8,128)S(1)} %get-tuple-element.19.keep) | copy-start | bytes 2359300
  52.6 1.9 %collective-permute-start.6 = (bf16[2,128,768]{2,1,0:T(8,128)(2,1)S(1)}, bf16[2,128,768]{2,1,0:T(8,128)(2,1)S(1)}, u32[]{:S(2)}, u32[]{:S(2)}) collective-permute-start(bf16[2,128,768]{2,1,0:T(8,128)(2,1)S(1)} %get-tuple-element.20), channel_id=1, source_target_pairs={{0,1},{1,0},{2,3},{3,2},{4,5},{5,4},{6,7},{7,6},{8,9},{9,8},{10,11... | collective-permute-start | bytes 1179656 | tf_op jit(solution)/shard_map/ppermute | solution.py:78
  57.2 8.2 %collective-permute-start.7 = (bf16[32,768]{1,0:T(8,128)(2,1)}, bf16[32,768]{1,0:T(8,128)(2,1)S(1)}, u32[]{:S(2)}, u32[]{:S(2)}) collective-permute-start(bf16[32,768]{1,0:T(8,128)(2,1)} %get-tuple-element.22), channel_id=1, source_target_pairs={{0,14},{1,15},{2,12},{3,13},{4,10},{5,11},{6,8},{7,9},{8,6},{9,7},... | collective-permute-start | bytes 147464 | tf_op jit(solution)/shard_map/ppermute | solution.py:78
  60.1 7.8 %collective-permute-start.8 = (bf16[32,768]{1,0:T(8,128)(2,1)}, bf16[32,768]{1,0:T(8,128)(2,1)S(1)}, u32[]{:S(2)}, u32[]{:S(2)}) collective-permute-start(bf16[32,768]{1,0:T(8,128)(2,1)} %get-tuple-element.23), channel_id=1, source_target_pairs={{0,12},{1,13},{2,14},{3,15},{4,8},{5,9},{6,10},{7,11},{8,4},{9,5},... | collective-permute-start | bytes 147464 | tf_op jit(solution)/shard_map/ppermute | solution.py:78
  62.1 7.0 %collective-permute-start.9 = (bf16[32,768]{1,0:T(8,128)(2,1)}, bf16[32,768]{1,0:T(8,128)(2,1)S(1)}, u32[]{:S(2)}, u32[]{:S(2)}) collective-permute-start(bf16[32,768]{1,0:T(8,128)(2,1)} %get-tuple-element.24), channel_id=1, source_target_pairs={{0,10},{1,11},{2,8},{3,9},{4,14},{5,15},{6,12},{7,13},{8,2},{9,3},... | collective-permute-start | bytes 147464 | tf_op jit(solution)/shard_map/ppermute | solution.py:78
  62.1 8.1 %collective-permute-start.10 = (bf16[32,768]{1,0:T(8,128)(2,1)}, bf16[32,768]{1,0:T(8,128)(2,1)S(1)}, u32[]{:S(2)}, u32[]{:S(2)}) collective-permute-start(bf16[32,768]{1,0:T(8,128)(2,1)} %get-tuple-element.25), channel_id=1, source_target_pairs={{0,8},{1,9},{2,10},{3,11},{4,12},{5,13},{6,14},{7,15},{8,0},{9,1},... | collective-permute-start | bytes 147464 | tf_op jit(solution)/shard_map/ppermute | solution.py:78
  64.9 5.7 %collective-permute-start.11 = (bf16[32,768]{1,0:T(8,128)(2,1)}, bf16[32,768]{1,0:T(8,128)(2,1)S(1)}, u32[]{:S(2)}, u32[]{:S(2)}) collective-permute-start(bf16[32,768]{1,0:T(8,128)(2,1)} %get-tuple-element.26), channel_id=1, source_target_pairs={{0,6},{1,7},{2,4},{3,5},{4,2},{5,3},{6,0},{7,1},{8,14},{9,15},{10,... | collective-permute-start | bytes 147464 | tf_op jit(solution)/shard_map/ppermute | solution.py:78
  65.4 6.9 %copy-start.8 = (bf16[32,768]{1,0:T(8,128)(2,1)}, bf16[32,768]{1,0:T(8,128)(2,1)S(1)}, u32[]{:S(2)}) copy-start(bf16[32,768]{1,0:T(8,128)(2,1)S(1)} %collective-permute-done.7.refs_1_) | copy-start | bytes 147460
  65.4 6.2 %collective-permute-start.12 = (bf16[32,768]{1,0:T(8,128)(2,1)}, bf16[32,768]{1,0:T(8,128)(2,1)S(1)}, u32[]{:S(2)}, u32[]{:S(2)}) collective-permute-start(bf16[32,768]{1,0:T(8,128)(2,1)} %get-tuple-element.27), channel_id=1, source_target_pairs={{0,4},{1,5},{2,6},{3,7},{4,0},{5,1},{6,2},{7,3},{8,12},{9,13},{10,... | collective-permute-start | bytes 147464 | tf_op jit(solution)/shard_map/ppermute | solution.py:78
  67.9 4.3 %copy-start.9 = (bf16[32,768]{1,0:T(8,128)(2,1)}, bf16[32,768]{1,0:T(8,128)(2,1)S(1)}, u32[]{:S(2)}) copy-start(bf16[32,768]{1,0:T(8,128)(2,1)S(1)} %collective-permute-done.8.refs_2_) | copy-start | bytes 147460
  67.9 4.3 %collective-permute-start.13 = (bf16[32,768]{1,0:T(8,128)(2,1)}, bf16[32,768]{1,0:T(8,128)(2,1)S(1)}, u32[]{:S(2)}, u32[]{:S(2)}) collective-permute-start(bf16[32,768]{1,0:T(8,128)(2,1)} %get-tuple-element.28), channel_id=1, source_target_pairs={{0,2},{1,3},{2,0},{3,1},{4,6},{5,7},{6,4},{7,5},{8,10},{9,11},{10,... | collective-permute-start | bytes 147464 | tf_op jit(solution)/shard_map/ppermute | solution.py:78
  69.1 3.2 %copy-start.10 = (bf16[32,768]{1,0:T(8,128)(2,1)}, bf16[32,768]{1,0:T(8,128)(2,1)S(1)}, u32[]{:S(2)}) copy-start(bf16[32,768]{1,0:T(8,128)(2,1)S(1)} %collective-permute-done.9.refs_3_) | copy-start | bytes 147460
  70.1 2.1 %copy-start.11 = (bf16[32,768]{1,0:T(8,128)(2,1)}, bf16[32,768]{1,0:T(8,128)(2,1)S(1)}, u32[]{:S(2)}) copy-start(bf16[32,768]{1,0:T(8,128)(2,1)S(1)} %collective-permute-done.10.refs_4_) | copy-start | bytes 147460
  70.5 1.7 %copy-start.12 = (bf16[32,768]{1,0:T(8,128)(2,1)}, bf16[32,768]{1,0:T(8,128)(2,1)S(1)}, u32[]{:S(2)}) copy-start(bf16[32,768]{1,0:T(8,128)(2,1)S(1)} %collective-permute-done.11.refs_5_) | copy-start | bytes 147460
  (5 other events, 3.3 us)

commit v2 on v0

--- a/solution.py
+++ b/solution.py
@@ -1,9 +1,20 @@
+import functools
+
 import jax
 import jax.numpy as jnp
 from jax import lax
+from jax.experimental import pallas as pl
+from jax.experimental.pallas import tpu as pltpu
 from jax.sharding import PartitionSpec as P
 
 EXPERTS = 4
+LANES = 128
+BF16 = jnp.bfloat16
+F32 = jnp.float32
+MIB = 1 << 20
+JOINT = ("expert", "hidden")
+VMEM = pl.BlockSpec(memory_space=pltpu.VMEM)
+HBM = pl.BlockSpec(memory_space=pltpu.HBM)
 
 
 def on_device(
@@ -60,6 +71,270 @@
     return mixed.astype(jnp.bfloat16)
 
 
+def swap(value, expert_bits, hidden_bits):
+    pairs = [
+        (e * 4 + h, (e ^ expert_bits) * 4 + (h ^ hidden_bits)) for e in range(4) for h in range(4)
+    ]
+    return lax.ppermute(value, JOINT, pairs)
+
+
+def in_vmem(array):
+    return pltpu.with_memory_space_constraint(array, pltpu.VMEM)
+
+
+def in_hbm(array):
+    return pltpu.with_memory_space_constraint(array, pltpu.HBM)
+
+
+def pack_body(tokens, router, routes, slots, out_ref, tok_ref, rw_ref, routes_ref, slots_ref, sem):
+    rows, width = tok_ref.shape
+    base = lax.axis_index("expert") * rows
+    moves = ((tokens, tok_ref), (router, rw_ref), (routes, routes_ref), (slots, slots_ref))
+    copies = [pltpu.make_async_copy(*move, sem.at[index]) for index, move in enumerate(moves)]
+    for copy in copies:
+        copy.start()
+    for copy in copies:
+        copy.wait()
+    out_ref[:, :width] = tok_ref[...]
+    values = tok_ref[...].astype(F32)
+    lane = lax.broadcasted_iota(jnp.int32, (rows, LANES), 1)
+    diagonal = lax.broadcasted_iota(jnp.int32, (rows, rows), 0) == lax.broadcasted_iota(
+        jnp.int32, (rows, rows), 1
+    )
+    meta = jnp.zeros((rows, LANES), F32)
+    for expert in range(EXPERTS):
+        logit = jnp.sum(values * rw_ref[expert : expert + 1, :], axis=1, keepdims=True)
+        high = logit.astype(BF16).astype(F32)
+        middle = (logit - high).astype(BF16).astype(F32)
+        low = logit - high - middle
+        code = jnp.zeros((1, rows), F32) - 1.0
+        for pick in range(2):
+            here = (slots_ref[pick : pick + 1, :] - base).astype(F32)
+            code = jnp.where(routes_ref[pick : pick + 1, :] == expert, here, code)
+        column = jnp.sum(jnp.where(diagonal, code, 0.0), axis=1, keepdims=True)
+        for place, term in enumerate((column, high, middle, low)):
+            meta = jnp.where(lane == place * EXPERTS + expert, term, meta)
+    out_ref[:, width:] = meta.astype(BF16)
+
+
+PACK_FLOPS = 24_000_000_000
+
+
+def pack(tokens, router_t, routes_t, slots_t):
+    rows, width = tokens.shape
+    arrays = [in_hbm(array) for array in (tokens, router_t, routes_t, slots_t)]
+    return pl.pallas_call(
+        pack_body,
+        in_specs=[HBM] * 4,
+        out_specs=VMEM,
+        out_shape=pltpu.VMEM((rows, width + LANES), BF16),
+        scratch_shapes=[pltpu.VMEM(array.shape, array.dtype) for array in arrays]
+        + [pltpu.SemaphoreType.DMA((4,))],
+        compiler_params=pltpu.CompilerParams(vmem_limit_bytes=4 * MIB),
+        cost_estimate=pl.CostEstimate(flops=PACK_FLOPS, bytes_accessed=0, transcendentals=0),
+        name="pack",
+    )(*arrays)
+
+
+def join_body(*refs):
+    out_ref = refs[-1]
+    rows = refs[0].shape[0]
+    for index, ref in enumerate(refs[:-1]):
+        out_ref[index * rows : (index + 1) * rows, :] = ref[...]
+
+
+def join(parts):
+    rows, width = parts[0].shape
+    return pl.pallas_call(
+        join_body,
+        in_specs=[VMEM] * len(parts),
+        out_specs=VMEM,
+        out_shape=pltpu.VMEM((rows * len(parts), width), BF16),
+        compiler_params=pltpu.CompilerParams(vmem_limit_bytes=4 * MIB),
+        name="join",
+    )(*parts)
+
+
+def place():
+    hidden = lax.axis_index("hidden")
+    return hidden // 2, hidden % 2
+
+
+TILE = 512
+
+
+def span(index, size):
+    return pl.ds(pl.multiple_of(index * size, size), size)
+
+
+SCOPE = 13 * MIB
+SLOTS = 6
+CUT = 1024
+SUB = 256
+
+
+def main_body(
+    own, mate, cross, cross_mate, expo, wg, wu, wd, send, keep, left, hid, limits, buf, sem
+):
+    chip, core = place()
+    expert = lax.axis_index("expert")
+    rows = own.shape[0]
+    width = own.shape[1] - LANES
+    slots = buf.shape[0]
+    cuts = hid.shape[1] // CUT
+
+    def owner(block):
+        to_chip = chip if block % 2 == 0 else 1 - chip
+        return 2 * to_chip + (1 - core if block < 2 else core)
+
+    def copy(unit):
+        part = wd.at[0, pl.ds(unit % cuts * CUT, CUT), span(owner(unit // cuts), width)]
+        return pltpu.make_async_copy(part, buf.at[unit % slots], sem.at[unit % slots])
+
+    for unit in range(slots):
+        copy(unit).start()
+
+    for to_chip, first, second in ((chip, own, mate), (1 - chip, cross, cross_mate)):
+        left[:, span(2 * to_chip + core, width)] = first[:, :width]
+        left[:, span(2 * to_chip + 1 - core, width)] = second[:, :width]
+
+    meta = own[:, width:].astype(F32)
+    lane = lax.broadcasted_iota(jnp.int32, meta.shape, 1)
+    terms = meta
+    for ref in (mate, cross, cross_mate):
+        terms = terms + ref[:, width:].astype(F32)
+    code = jnp.sum(jnp.where(lane == expert, meta, 0.0), axis=1, keepdims=True)
+    first = jnp.zeros((rows, 1), F32)
+    other = jnp.zeros((rows, 1), F32)
+    for index in range(EXPERTS):
+        used = (lane >= EXPERTS) & (lane < 4 * EXPERTS) & (lax.rem(lane, EXPERTS) == index)
+        logit = jnp.sum(jnp.where(used, terms, 0.0), axis=1, keepdims=True)
+        routed = meta[:, index : index + 1] >= 0.0
+        first = jnp.where(index == expert, logit, first)
+        other = jnp.where(routed & (index != expert), logit, other)
+    weight = jnp.where(code >= 0.0, 1.0 / (1.0 + jnp.exp(other - first)), 0.0)
+    slots_each = rows // EXPERTS
+    row = lax.broadcasted_iota(jnp.int32, (rows, rows), 0)
+    source = jnp.bitwise_xor(row // slots_each, expert)
+    target = jnp.where(code >= 0.0, (source * slots_each).astype(F32) + code, -1.0)
+    chosen = lax.broadcasted_iota(jnp.int32, (rows, rows), 1).astype(F32) == target
+    table = 448.0 * jnp.exp2(-expo[...].astype(F32))
+    limits[...] = lax.dot_general(
+        chosen.astype(BF16), table.astype(BF16), (((1,), (1,)), ((), ())), preferred_element_type=F32
+    )
+
+    @pl.loop(0, wg.shape[1] // TILE)
+    def _(index):
+        for sub in range(TILE // SUB):
+            columns = span(index * (TILE // SUB) + sub, SUB)
+            gate = jnp.dot(left[...], wg[:, columns], preferred_element_type=F32)
+            up = jnp.dot(left[...], wu[:, columns], preferred_element_type=F32)
+            hid[:, columns] = (gate / (1.0 + jnp.exp(-gate)) * up).astype(BF16)
+
+    unit = 0
+    for block in range(4):
+        partial = None
+        for cut in range(cuts):
+            copy(unit).wait()
+            term = jnp.dot(
+                hid[:, cut * CUT : (cut + 1) * CUT], buf[unit % slots], preferred_element_type=F32
+            )
+            partial = term if partial is None else partial + term
+            if unit + slots < 4 * cuts:
+                copy(unit + slots).start()
+            unit += 1
+        out = (send, keep)[block // 2]
+        blocks = lax.broadcasted_iota(jnp.int32, limits.shape, 1)
+        for piece in range(width // LANES):
+            columns = slice(piece * LANES, (piece + 1) * LANES)
+            feature = owner(block) * (width // LANES) + piece
+            bound = jnp.sum(jnp.where(blocks == feature, limits[...], 0.0), axis=1, keepdims=True)
+            coded = jnp.clip(partial[:, columns], -bound, bound).astype(BF16).astype(F32)
+            out[block % 2, :, columns] = (coded * weight).astype(out.dtype)
+
+
+def main(own, mate, cross, cross_mate, expo, wg, wu, wd):
+    rows, width = own.shape
+    width = width - LANES
+    depth, units = wg.shape
+    return pl.pallas_call(
+        main_body,
+        in_specs=[VMEM] * 7 + [HBM],
+        out_specs=[VMEM, VMEM],
+        out_shape=[pltpu.VMEM((2, rows, width), BF16), pltpu.VMEM((2, rows, width), F32)],
+        scratch_shapes=[
+            pltpu.VMEM((rows, depth), BF16),
+            pltpu.VMEM((rows, units), BF16),
+            pltpu.VMEM((rows, expo.shape[0]), F32),
+            pltpu.VMEM((SLOTS, CUT, width), BF16),
+            pltpu.SemaphoreType.DMA((SLOTS,)),
+        ],
+        cost_estimate=pl.CostEstimate(
+            flops=6 * rows * depth * units, bytes_accessed=6 * depth * units, transcendentals=0
+        ),
+        compiler_params=pltpu.CompilerParams(vmem_limit_bytes=SCOPE),
+        name="main",
+    )(own, mate, cross, cross_mate, expo, wg, wu, wd)
+
+
+def split_body(keep, got, *outs):
+    rows = outs[0].shape[0]
+    for index, out in enumerate(outs):
+        chip, block = index // EXPERTS, index % EXPERTS
+        piece = slice(block * rows, (block + 1) * rows)
+        out[...] = (keep[chip, piece, :] + got[chip, piece, :].astype(F32)).astype(out.dtype)
+
+
+def split(keep, got):
+    rows, width = keep.shape[1] // EXPERTS, keep.shape[2]
+    kinds = [F32] + [BF16] * (2 * EXPERTS - 1)
+    return pl.pallas_call(
+        split_body,
+        in_specs=[VMEM, VMEM],
+        out_specs=[VMEM] * len(kinds),
+        out_shape=[jax.ShapeDtypeStruct((rows, width), kind) for kind in kinds],
+        compiler_params=pltpu.CompilerParams(vmem_limit_bytes=4 * MIB),
+        name="split",
+    )(keep, got)
+
+
+def total_body(*refs):
+    total = refs[0][...]
+    for ref in refs[1:-1]:
+        total = total + ref[...].astype(F32)
+    refs[-1][...] = total.astype(BF16)
+
+
+def total(parts):
+    return pl.pallas_call(
+        total_body,
+        in_specs=[VMEM] * len(parts),
+        out_specs=VMEM,
+        out_shape=jax.ShapeDtypeStruct(parts[0].shape, BF16),
+        compiler_params=pltpu.CompilerParams(vmem_limit_bytes=4 * MIB),
+        name="total",
+    )(*parts)
+
+
+def fast(tokens, router_weight, routes, slots, gate_weight, up_weight, down_weight, scale_exponents):
+    packed = pack(tokens, router_weight.T, routes.T, slots.T)
+    own = in_vmem(join([packed] + [swap(packed, bits, 0) for bits in (1, 2, 3)]))
+    mate = in_vmem(swap(own, 0, 1))
+    cross = in_vmem(swap(own, 0, 2))
+    cross_mate = in_vmem(swap(cross, 0, 1))
+    send, keep = main(
+        own, mate, cross, cross_mate, in_vmem(scale_exponents[0, 0].T),
+        in_vmem(gate_weight[0]), in_vmem(up_weight[0]), in_hbm(down_weight),
+    )
+    blocks = split(in_vmem(keep), in_vmem(swap(send, 0, 1)))
+    parts = [blocks[0]]
+    for bits in (3, 2, 1):
+        for chip in (2, 0):
+            parts.append(swap(blocks[(chip // 2) * EXPERTS + bits], bits, chip))
+    parts.append(swap(blocks[EXPERTS], 0, 2))
+    return total(parts)
+
+
 def solution(mesh):
     placed = (
         P(("groups", "expert"), "hidden"),
@@ -71,8 +346,9 @@
         P("expert", "hidden", None),
         P(("groups", "expert"), "hidden", None, None),
     )
+    general = mesh.shape["expert"] != 4 or mesh.shape["hidden"] != 4
     return jax.shard_map(
-        on_device,
+        on_device if general else fast,
         mesh=mesh,
         in_specs=placed,
         out_specs=P(("groups", "expert"), "hidden"),

time: 135 us -> 54.5 us (0.40)
  matrix products: 37.9 us -> 0 us
  local copies, waits for them, and re-layouts: 32.9 us -> 0.01 us
  Pallas kernels: 0 us -> 19.3 us
  blocking collectives: 13.9 us -> 0 us
  between operations: 13.5 us -> 0.04 us
  starting transfers between devices: 9.68 us -> 18.8 us
  waiting for transfers between devices: 25 us -> 16.3 us
  other arithmetic: 1.44 us -> 0 us
    dot_general x8 -> x0, matrix products: 37.9 us -> none  [the longest x1 12.7 us: on_device(): jnp.dot(hidden, down_weight[0], preferred_element_type=jnp.float32)]
    dot_general x1 -> x0, local copies, waits for them, and re-layouts: 30.8 us -> none  [on_device(): jnp.dot(hidden, down_weight[0], preferred_element_type=jnp.float32)]
    pallas_call x0 -> x5, Pallas kernels: none -> 19.3 us  [the longest x1 17.4 us: main(): pl.pallas_call(main_body, in_specs=[VMEM] * 7 + [HBM], out_specs=[VMEM, V...]
    ppermute x0 -> x14, starting transfers between devices: none -> 18.8 us  [swap(): return lax.ppermute(value, JOINT, pairs)]
    reduce_scatter x1 -> x0, waiting for transfers between devices: 17.8 us -> none  [on_device(): lax.psum_scatter(coded.astype(jnp.float32).astype(jnp.bfloat16), 'hidden'...]
    ppermute x0 -> x14, waiting for transfers between devices: none -> 16.3 us  [swap(): return lax.ppermute(value, JOINT, pairs)]
    all_to_all x2 -> x0, starting transfers between devices: 9.67 us -> none  [the longest x1 5.09 us: on_device(): lax.all_to_all(outgoing, 'expert', split_axis=0, concat_axis=0, tiled=True)]
    all_to_all x2 -> x0, waiting for transfers between devices: 7.11 us -> none  [the longest x1 7.11 us: on_device(): lax.all_to_all(quarter_out, 'expert', split_axis=0, concat_axis=0, tiled=...]
  transfers between devices with their start and end apart: 3 -> 14, of which waited for: 2 -> 10; matrix products, arithmetic and copies ran while one was open for 23% -> 0% of each run, Pallas kernels for 0% -> 0%
where the time goes in v2:
time: 54.5 us; the launch traced here: 54.4 us
  Pallas kernels  19.3 us (35%)
  starting transfers between devices  18.8 us (34%)
  waiting for transfers between devices  16.3 us (30%)
    ppermute x14, starting transfers between devices, swap(): return lax.ppermute(value, JOINT, pairs)  18.8 us
    pallas_call x1, Pallas kernels, main(): pl.pallas_call(main_body, in_specs=[VMEM] * 7 + [HBM], out_specs=[VMEM, V...  17.4 us
    ppermute x14, waiting for transfers between devices, swap(): return lax.ppermute(value, JOINT, pairs)  16.3 us
    pallas_call x1, Pallas kernels, pack(): pl.pallas_call(pack_body, in_specs=[HBM] * 4, out_specs=VMEM, out_shape=p...  1.11 us
  transfers between devices with their start and end apart: 14, of which 10 were waited for; matrix products, arithmetic and copies ran while one was open for 0% of the time, Pallas kernels for 0%

profile of v2, /device:TPU:0, one launch (start us, length us, event | category | flops | bytes accessed | tf_op | source)
XLA Modules:
  0.0 54.4 jit_solution(15313285270783468332)
XLA Ops:
  0.0 1.1 %pack.1.refs_0_ = bf16[32,896]{1,0:T(8,128)(2,1)S(1)} custom-call(bf16[32,768]{1,0:T(8,128)(2,1)} %tokens.1, f32[4,768]{1,0:T(4,128)} %bitcast.11, s32[2,32]{1,0:T(2,128)} %bitcast.12, s32[2,32]{1,0:T(2,128)} %bitcast.13), custom_call_target="tpu_custom_call" | custom-call | flops 24000000000 | tf_op jit(solution)/shard_map/pack/pallas_call | solution.py:126
  1.1 5.1 %collective-permute-start.2 = (bf16[32,896]{1,0:T(8,128)(2,1)S(1)}, bf16[32,896]{1,0:T(8,128)(2,1)S(1)}, u32[]{:S(2)}, u32[]{:S(2)}) collective-permute-start(bf16[32,896]{1,0:T(8,128)(2,1)S(1)} %pack.1.refs_0_), channel_id=1, source_target_pairs={{0,12},{1,13},{2,14},{3,15},{4,8},{5,9},{6,10},{7,11},{8,4},{9,5},... | collective-permute-start | bytes 172040 | tf_op jit(solution)/shard_map/ppermute | solution.py:78
  6.2 0.6 %collective-permute-start = (bf16[32,896]{1,0:T(8,128)(2,1)S(1)}, bf16[32,896]{1,0:T(8,128)(2,1)S(1)}, u32[]{:S(2)}, u32[]{:S(2)}) collective-permute-start(bf16[32,896]{1,0:T(8,128)(2,1)S(1)} %pack.1.refs_0_), channel_id=1, source_target_pairs={{0,4},{1,5},{2,6},{3,7},{4,0},{5,1},{6,2},{7,3},{8,12},{9,13},{10,... | collective-permute-start | bytes 172040 | tf_op jit(solution)/shard_map/ppermute | solution.py:78
  6.9 1.8 %collective-permute-done.2.refs_3_ = bf16[32,896]{1,0:T(8,128)(2,1)S(1)} collective-permute-done((bf16[32,896]{1,0:T(8,128)(2,1)S(1)}, bf16[32,896]{1,0:T(8,128)(2,1)S(1)}, u32[]{:S(2)}, u32[]{:S(2)}) %collective-permute-start.2) | collective-permute-done | bytes 57376 | tf_op jit(solution)/shard_map/ppermute | solution.py:78
  8.7 2.7 %collective-permute-done.1.refs_2_ = bf16[32,896]{1,0:T(8,128)(2,1)S(1)} collective-permute-done((bf16[32,896]{1,0:T(8,128)(2,1)S(1)}, bf16[32,896]{1,0:T(8,128)(2,1)S(1)}, u32[]{:S(2)}, u32[]{:S(2)}) %collective-permute-start.1) | collective-permute-done | bytes 57376 | tf_op jit(solution)/shard_map/ppermute | solution.py:78
  11.3 1.6 %collective-permute-start.4 = (bf16[128,896]{1,0:T(8,128)(2,1)S(1)}, bf16[128,896]{1,0:T(8,128)(2,1)S(1)}, u32[]{:S(2)}, u32[]{:S(2)}) collective-permute-start(bf16[128,896]{1,0:T(8,128)(2,1)S(1)} %join.1.own), channel_id=1, source_target_pairs={{0,2},{1,3},{2,0},{3,1},{4,6},{5,7},{6,4},{7,5},{8,10},{9,11},{10,... | collective-permute-start | bytes 688136 | tf_op jit(solution)/shard_map/ppermute | solution.py:78
  12.9 5.1 %collective-permute-done.4.cross = bf16[128,896]{1,0:T(8,128)(2,1)S(1)} collective-permute-done((bf16[128,896]{1,0:T(8,128)(2,1)S(1)}, bf16[128,896]{1,0:T(8,128)(2,1)S(1)}, u32[]{:S(2)}, u32[]{:S(2)}) %collective-permute-start.4) | collective-permute-done | bytes 229408 | tf_op jit(solution)/shard_map/ppermute | solution.py:78
  18.1 1.5 %collective-permute-done.5.cross_mate = bf16[128,896]{1,0:T(8,128)(2,1)S(1)} collective-permute-done((bf16[128,896]{1,0:T(8,128)(2,1)S(1)}, bf16[128,896]{1,0:T(8,128)(2,1)S(1)}, u32[]{:S(2)}, u32[]{:S(2)}) %collective-permute-start.5) | collective-permute-done | bytes 229408 | tf_op jit(solution)/shard_map/ppermute | solution.py:78
  19.6 17.4 %main.1 = (bf16[2,128,768]{2,1,0:T(8,128)(2,1)S(1)}, f32[2,128,768]{2,1,0:T(8,128)S(1)}) custom-call(bf16[128,896]{1,0:T(8,128)(2,1)S(1)} %join.1.own, bf16[128,896]{1,0:T(8,128)(2,1)S(1)} %collective-permute-done.3.mate, bf16[128,896]{1,0:T(8,128)(2,1)S(1)} %collective-permute-done.4.cross, bf16[128,896]{1,0:T(8,128)(2,1)S(1)} %collective-permute-done.5.cross_mate, ...), custom_call_target="tpu_custom_call" | custom-call | flops 9663676416 | bytes 75497472 | tf_op jit(solution)/shard_map/main/pallas_call | solution.py:260
  37.0 0.2 collective-permute-start.6
  37.2 1.6 %collective-permute-done.6.got = bf16[2,128,768]{2,1,0:T(8,128)(2,1)S(1)} collective-permute-done((bf16[2,128,768]{2,1,0:T(8,128)(2,1)S(1)}, bf16[2,128,768]{2,1,0:T(8,128)(2,1)S(1)}, u32[]{:S(2)}, u32[]{:S(2)}) %collective-permute-start.6) | collective-permute-done | bytes 393248 | tf_op jit(solution)/shard_map/ppermute | solution.py:78
  38.8 0.1 split.1
  38.9 3.2 %collective-permute-start.7 = (bf16[32,768]{1,0:T(8,128)(2,1)S(1)}, bf16[32,768]{1,0:T(8,128)(2,1)S(1)}, u32[]{:S(2)}, u32[]{:S(2)}) collective-permute-start(bf16[32,768]{1,0:T(8,128)(2,1)S(1)} %get-tuple-element.18), channel_id=1, source_target_pairs={{0,14},{1,15},{2,12},{3,13},{4,10},{5,11},{6,8},{7,9},{8,6},{9,7},... | collective-permute-start | bytes 147464 | tf_op jit(solution)/shard_map/ppermute | solution.py:78
  42.0 1.8 %collective-permute-start.8 = (bf16[32,768]{1,0:T(8,128)(2,1)S(1)}, bf16[32,768]{1,0:T(8,128)(2,1)S(1)}, u32[]{:S(2)}, u32[]{:S(2)}) collective-permute-start(bf16[32,768]{1,0:T(8,128)(2,1)S(1)} %get-tuple-element.19), channel_id=1, source_target_pairs={{0,12},{1,13},{2,14},{3,15},{4,8},{5,9},{6,10},{7,11},{8,4},{9,5},... | collective-permute-start | bytes 147464 | tf_op jit(solution)/shard_map/ppermute | solution.py:78
  43.8 2.8 %collective-permute-start.10 = (bf16[32,768]{1,0:T(8,128)(2,1)S(1)}, bf16[32,768]{1,0:T(8,128)(2,1)S(1)}, u32[]{:S(2)}, u32[]{:S(2)}) collective-permute-start(bf16[32,768]{1,0:T(8,128)(2,1)S(1)} %get-tuple-element.21), channel_id=1, source_target_pairs={{0,8},{1,9},{2,10},{3,11},{4,12},{5,13},{6,14},{7,15},{8,0},{9,1},... | collective-permute-start | bytes 147464 | tf_op jit(solution)/shard_map/ppermute | solution.py:78
  46.6 0.7 %collective-permute-start.11 = (bf16[32,768]{1,0:T(8,128)(2,1)S(1)}, bf16[32,768]{1,0:T(8,128)(2,1)S(1)}, u32[]{:S(2)}, u32[]{:S(2)}) collective-permute-start(bf16[32,768]{1,0:T(8,128)(2,1)S(1)} %get-tuple-element.22), channel_id=1, source_target_pairs={{0,6},{1,7},{2,4},{3,5},{4,2},{5,3},{6,0},{7,1},{8,14},{9,15},{10,... | collective-permute-start | bytes 147464 | tf_op jit(solution)/shard_map/ppermute | solution.py:78
  47.3 2.3 %collective-permute-start.12 = (bf16[32,768]{1,0:T(8,128)(2,1)S(1)}, bf16[32,768]{1,0:T(8,128)(2,1)S(1)}, u32[]{:S(2)}, u32[]{:S(2)}) collective-permute-start(bf16[32,768]{1,0:T(8,128)(2,1)S(1)} %get-tuple-element.23), channel_id=1, source_target_pairs={{0,4},{1,5},{2,6},{3,7},{4,0},{5,1},{6,2},{7,3},{8,12},{9,13},{10,... | collective-permute-start | bytes 147464 | tf_op jit(solution)/shard_map/ppermute | solution.py:78
  49.6 0.4 collective-permute-start.13
  50.1 0.5 %collective-permute-done.9.refs_3_ = bf16[32,768]{1,0:T(8,128)(2,1)S(1)} collective-permute-done((bf16[32,768]{1,0:T(8,128)(2,1)S(1)}, bf16[32,768]{1,0:T(8,128)(2,1)S(1)}, u32[]{:S(2)}, u32[]{:S(2)}) %collective-permute-start.9) | collective-permute-done | bytes 49184 | tf_op jit(solution)/shard_map/ppermute | solution.py:78
  50.6 0.9 %collective-permute-done.10.refs_4_ = bf16[32,768]{1,0:T(8,128)(2,1)S(1)} collective-permute-done((bf16[32,768]{1,0:T(8,128)(2,1)S(1)}, bf16[32,768]{1,0:T(8,128)(2,1)S(1)}, u32[]{:S(2)}, u32[]{:S(2)}) %collective-permute-start.10) | collective-permute-done | bytes 49184 | tf_op jit(solution)/shard_map/ppermute | solution.py:78
  51.6 0.5 collective-permute-done.11.refs_5_
  52.1 1.0 %collective-permute-done.12.refs_6_ = bf16[32,768]{1,0:T(8,128)(2,1)S(1)} collective-permute-done((bf16[32,768]{1,0:T(8,128)(2,1)S(1)}, bf16[32,768]{1,0:T(8,128)(2,1)S(1)}, u32[]{:S(2)}, u32[]{:S(2)}) %collective-permute-start.12) | collective-permute-done | bytes 49184 | tf_op jit(solution)/shard_map/ppermute | solution.py:78
  53.1 0.6 %collective-permute-done.13.refs_7_ = bf16[32,768]{1,0:T(8,128)(2,1)S(1)} collective-permute-done((bf16[32,768]{1,0:T(8,128)(2,1)S(1)}, bf16[32,768]{1,0:T(8,128)(2,1)S(1)}, u32[]{:S(2)}, u32[]{:S(2)}) %collective-permute-start.13) | collective-permute-done | bytes 49184 | tf_op jit(solution)/shard_map/ppermute | solution.py:78
  53.7 0.7 %total.1 = bf16[32,768]{1,0:T(8,128)(2,1)} custom-call(f32[32,768]{1,0:T(8,128)S(1)} %get-tuple-element.17.refs_0_, bf16[32,768]{1,0:T(8,128)(2,1)S(1)} %collective-permute-done.7.refs_1_, bf16[32,768]{1,0:T(8,128)(2,1)S(1)} %collective-permute-done.8.refs_2_, bf16[32,768]{1,0:T(8,128)(2,1)S(1)} %collective-permute-done.9.refs_3_, ...), custom_call_target="tpu_custom_call" | custom-call | tf_op jit(solution)/shard_map/total/pallas_call | solution.py:309
  (15 shorter events, 0.0 us)
Async XLA Ops:
  0.0 19.5 %copy-start = (bf16[1,3072,4096]{2,1,0:T(8,128)(2,1)S(1)}, bf16[1,3072,4096]{2,1,0:T(8,128)(2,1)}, u32[]{:S(2)}) copy-start(bf16[1,3072,4096]{2,1,0:T(8,128)(2,1)} %param.12) | copy-start | bytes 75497472
  0.0 19.5 %copy-start.1 = (bf16[1,3072,4096]{2,1,0:T(8,128)(2,1)S(1)}, bf16[1,3072,4096]{2,1,0:T(8,128)(2,1)}, u32[]{:S(2)}) copy-start(bf16[1,3072,4096]{2,1,0:T(8,128)(2,1)} %param.13) | copy-start | bytes 75497472
  0.0 19.6 %copy-start.2 = (s32[1,1,128,24]{2,3,1,0:T(8,128)S(1)}, s32[1,1,128,24]{2,3,1,0:T(8,128)}, u32[]{:S(2)}) copy-start(s32[1,1,128,24]{2,3,1,0:T(8,128)} %param.15) | copy-start | bytes 36868
  1.1 7.5 %collective-permute-start.2 = (bf16[32,896]{1,0:T(8,128)(2,1)S(1)}, bf16[32,896]{1,0:T(8,128)(2,1)S(1)}, u32[]{:S(2)}, u32[]{:S(2)}) collective-permute-start(bf16[32,896]{1,0:T(8,128)(2,1)S(1)} %pack.1.refs_0_), channel_id=1, source_target_pairs={{0,12},{1,13},{2,14},{3,15},{4,8},{5,9},{6,10},{7,11},{8,4},{9,5},... | collective-permute-start | bytes 172040 | tf_op jit(solution)/shard_map/ppermute | solution.py:78
  6.2 5.1 %collective-permute-start.1 = (bf16[32,896]{1,0:T(8,128)(2,1)S(1)}, bf16[32,896]{1,0:T(8,128)(2,1)S(1)}, u32[]{:S(2)}, u32[]{:S(2)}) collective-permute-start(bf16[32,896]{1,0:T(8,128)(2,1)S(1)} %pack.1.refs_0_), channel_id=1, source_target_pairs={{0,8},{1,9},{2,10},{3,11},{4,12},{5,13},{6,14},{7,15},{8,0},{9,1},... | collective-permute-start | bytes 172040 | tf_op jit(solution)/shard_map/ppermute | solution.py:78
  6.2 5.1 %collective-permute-start = (bf16[32,896]{1,0:T(8,128)(2,1)S(1)}, bf16[32,896]{1,0:T(8,128)(2,1)S(1)}, u32[]{:S(2)}, u32[]{:S(2)}) collective-permute-start(bf16[32,896]{1,0:T(8,128)(2,1)S(1)} %pack.1.refs_0_), channel_id=1, source_target_pairs={{0,4},{1,5},{2,6},{3,7},{4,0},{5,1},{6,2},{7,3},{8,12},{9,13},{10,... | collective-permute-start | bytes 172040 | tf_op jit(solution)/shard_map/ppermute | solution.py:78
  11.3 6.7 %collective-permute-start.4 = (bf16[128,896]{1,0:T(8,128)(2,1)S(1)}, bf16[128,896]{1,0:T(8,128)(2,1)S(1)}, u32[]{:S(2)}, u32[]{:S(2)}) collective-permute-start(bf16[128,896]{1,0:T(8,128)(2,1)S(1)} %join.1.own), channel_id=1, source_target_pairs={{0,2},{1,3},{2,0},{3,1},{4,6},{5,7},{6,4},{7,5},{8,10},{9,11},{10,... | collective-permute-start | bytes 688136 | tf_op jit(solution)/shard_map/ppermute | solution.py:78
  12.9 5.1 %collective-permute-start.3 = (bf16[128,896]{1,0:T(8,128)(2,1)S(1)}, bf16[128,896]{1,0:T(8,128)(2,1)S(1)}, u32[]{:S(2)}, u32[]{:S(2)}) collective-permute-start(bf16[128,896]{1,0:T(8,128)(2,1)S(1)} %join.1.own), channel_id=1, source_target_pairs={{0,1},{1,0},{2,3},{3,2},{4,5},{5,4},{6,7},{7,6},{8,9},{9,8},{10,11... | collective-permute-start | bytes 688136 | tf_op jit(solution)/shard_map/ppermute | solution.py:78
  18.1 1.5 %collective-permute-start.5 = (bf16[128,896]{1,0:T(8,128)(2,1)S(1)}, bf16[128,896]{1,0:T(8,128)(2,1)S(1)}, u32[]{:S(2)}, u32[]{:S(2)}) collective-permute-start(bf16[128,896]{1,0:T(8,128)(2,1)S(1)} %collective-permute-done.4.cross), channel_id=1, source_target_pairs={{0,1},{1,0},{2,3},{3,2},{4,5},{5,4},{6,7},{7,6},{8,9},{9,8},{10,11... | collective-permute-start | bytes 688136 | tf_op jit(solution)/shard_map/ppermute | solution.py:78
  37.0 1.8 %collective-permute-start.6 = (bf16[2,128,768]{2,1,0:T(8,128)(2,1)S(1)}, bf16[2,128,768]{2,1,0:T(8,128)(2,1)S(1)}, u32[]{:S(2)}, u32[]{:S(2)}) collective-permute-start(bf16[2,128,768]{2,1,0:T(8,128)(2,1)S(1)} %get-tuple-element.16), channel_id=1, source_target_pairs={{0,1},{1,0},{2,3},{3,2},{4,5},{5,4},{6,7},{7,6},{8,9},{9,8},{10,11... | collective-permute-start | bytes 1179656 | tf_op jit(solution)/shard_map/ppermute | solution.py:78
  38.9 8.4 %collective-permute-start.7 = (bf16[32,768]{1,0:T(8,128)(2,1)S(1)}, bf16[32,768]{1,0:T(8,128)(2,1)S(1)}, u32[]{:S(2)}, u32[]{:S(2)}) collective-permute-start(bf16[32,768]{1,0:T(8,128)(2,1)S(1)} %get-tuple-element.18), channel_id=1, source_target_pairs={{0,14},{1,15},{2,12},{3,13},{4,10},{5,11},{6,8},{7,9},{8,6},{9,7},... | collective-permute-start | bytes 147464 | tf_op jit(solution)/shard_map/ppermute | solution.py:78
  42.0 7.6 %collective-permute-start.8 = (bf16[32,768]{1,0:T(8,128)(2,1)S(1)}, bf16[32,768]{1,0:T(8,128)(2,1)S(1)}, u32[]{:S(2)}, u32[]{:S(2)}) collective-permute-start(bf16[32,768]{1,0:T(8,128)(2,1)S(1)} %get-tuple-element.19), channel_id=1, source_target_pairs={{0,12},{1,13},{2,14},{3,15},{4,8},{5,9},{6,10},{7,11},{8,4},{9,5},... | collective-permute-start | bytes 147464 | tf_op jit(solution)/shard_map/ppermute | solution.py:78
  43.8 6.8 %collective-permute-start.9 = (bf16[32,768]{1,0:T(8,128)(2,1)S(1)}, bf16[32,768]{1,0:T(8,128)(2,1)S(1)}, u32[]{:S(2)}, u32[]{:S(2)}) collective-permute-start(bf16[32,768]{1,0:T(8,128)(2,1)S(1)} %get-tuple-element.20), channel_id=1, source_target_pairs={{0,10},{1,11},{2,8},{3,9},{4,14},{5,15},{6,12},{7,13},{8,2},{9,3},... | collective-permute-start | bytes 147464 | tf_op jit(solution)/shard_map/ppermute | solution.py:78
  43.8 7.8 %collective-permute-start.10 = (bf16[32,768]{1,0:T(8,128)(2,1)S(1)}, bf16[32,768]{1,0:T(8,128)(2,1)S(1)}, u32[]{:S(2)}, u32[]{:S(2)}) collective-permute-start(bf16[32,768]{1,0:T(8,128)(2,1)S(1)} %get-tuple-element.21), channel_id=1, source_target_pairs={{0,8},{1,9},{2,10},{3,11},{4,12},{5,13},{6,14},{7,15},{8,0},{9,1},... | collective-permute-start | bytes 147464 | tf_op jit(solution)/shard_map/ppermute | solution.py:78
  46.6 5.5 %collective-permute-start.11 = (bf16[32,768]{1,0:T(8,128)(2,1)S(1)}, bf16[32,768]{1,0:T(8,128)(2,1)S(1)}, u32[]{:S(2)}, u32[]{:S(2)}) collective-permute-start(bf16[32,768]{1,0:T(8,128)(2,1)S(1)} %get-tuple-element.22), channel_id=1, source_target_pairs={{0,6},{1,7},{2,4},{3,5},{4,2},{5,3},{6,0},{7,1},{8,14},{9,15},{10,... | collective-permute-start | bytes 147464 | tf_op jit(solution)/shard_map/ppermute | solution.py:78
  47.3 5.8 %collective-permute-start.12 = (bf16[32,768]{1,0:T(8,128)(2,1)S(1)}, bf16[32,768]{1,0:T(8,128)(2,1)S(1)}, u32[]{:S(2)}, u32[]{:S(2)}) collective-permute-start(bf16[32,768]{1,0:T(8,128)(2,1)S(1)} %get-tuple-element.23), channel_id=1, source_target_pairs={{0,4},{1,5},{2,6},{3,7},{4,0},{5,1},{6,2},{7,3},{8,12},{9,13},{10,... | collective-permute-start | bytes 147464 | tf_op jit(solution)/shard_map/ppermute | solution.py:78
  49.6 4.1 %collective-permute-start.13 = (bf16[32,768]{1,0:T(8,128)(2,1)S(1)}, bf16[32,768]{1,0:T(8,128)(2,1)S(1)}, u32[]{:S(2)}, u32[]{:S(2)}) collective-permute-start(bf16[32,768]{1,0:T(8,128)(2,1)S(1)} %get-tuple-element.24), channel_id=1, source_target_pairs={{0,2},{1,3},{2,0},{3,1},{4,6},{5,7},{6,4},{7,5},{8,10},{9,11},{10,... | collective-permute-start | bytes 147464 | tf_op jit(solution)/shard_map/ppermute | solution.py:78

commit v3 on v2

--- a/solution.py
+++ b/solution.py
@@ -117,7 +117,7 @@
     out_ref[:, width:] = meta.astype(BF16)
 
 
-PACK_FLOPS = 24_000_000_000
+PACK_FLOPS = 12_000_000_000
 
 
 def pack(tokens, router_t, routes_t, slots_t):
@@ -167,36 +167,114 @@
     return pl.ds(pl.multiple_of(index * size, size), size)
 
 
-SCOPE = 13 * MIB
-SLOTS = 6
-CUT = 1024
+def fill_left(left, first, second, core, width):
+    left[:, pl.ds(pl.multiple_of(core * width, LANES), width)] = first[:, :width]
+    left[:, pl.ds(pl.multiple_of((1 - core) * width, LANES), width)] = second[:, :width]
+
+
+FETCH_COST = pl.CostEstimate(flops=5_000_000_000, bytes_accessed=0, transcendentals=0)
+SCOPE = 18 * MIB
+SLOTS = 4
+CUT = 512
 SUB = 256
 
 
-def main_body(
-    own, mate, cross, cross_mate, expo, wg, wu, wd, send, keep, left, hid, limits, buf, sem
+def fetch_body(wu, out, sem):
+    chip, _ = place()
+    copy = pltpu.make_async_copy(wu.at[0, span(chip, out.shape[0])], out, sem)
+    copy.start()
+    copy.wait()
+
+
+def fetch(wu):
+    return pl.pallas_call(
+        fetch_body,
+        in_specs=[HBM],
+        out_specs=VMEM,
+        out_shape=pltpu.VMEM((wu.shape[1] // 2, wu.shape[2]), BF16),
+        scratch_shapes=[pltpu.SemaphoreType.DMA],
+        cost_estimate=FETCH_COST,
+        compiler_params=pltpu.CompilerParams(vmem_limit_bytes=SCOPE),
+        name="fetch",
+    )(wu)
+
+
+def near_body(own, mate, expo, wg, up_near, wu, acc_g, acc_u, limits, up_far, left, sem):
+    chip, core = place()
+    rows = own.shape[0]
+    width = own.shape[1] - LANES
+    depth = 2 * width
+    fill_left(left, own, mate, core, width)
+    copies = []
+    for index in range(up_near.shape[1] // TILE):
+        columns = slice(index * TILE, (index + 1) * TILE)
+        acc_u[:, columns] = jnp.dot(left[...], up_near[:, columns], preferred_element_type=F32)
+        there = wu.at[0, span(1 - chip, depth), pl.ds(index * TILE, TILE)]
+        copies.append(pltpu.make_async_copy(there, up_far.at[:, columns], sem.at[index]))
+        copies[-1].start()
+        acc_g[:, columns] = jnp.dot(
+            left[...], wg[span(chip, depth), columns], preferred_element_type=F32
+        )
+
+    expert = lax.axis_index("expert")
+    meta = own[:, width:].astype(F32)
+    lane = lax.broadcasted_iota(jnp.int32, meta.shape, 1)
+    code = jnp.sum(jnp.where(lane == expert, meta, 0.0), axis=1, keepdims=True)
+    slots_each = rows // EXPERTS
+    row = lax.broadcasted_iota(jnp.int32, (rows, rows), 0)
+    source = jnp.bitwise_xor(row // slots_each, expert)
+    target = jnp.where(code >= 0.0, (source * slots_each).astype(F32) + code, -1.0)
+    chosen = lax.broadcasted_iota(jnp.int32, (rows, rows), 1).astype(F32) == target
+    table = 448.0 * jnp.exp2(-expo[...].astype(F32))
+    limits[...] = lax.dot_general(
+        chosen.astype(BF16), table.astype(BF16), (((1,), (1,)), ((), ())), preferred_element_type=F32
+    )
+    for copy in copies:
+        copy.wait()
+
+
+def near(own, mate, expo, wg, up_near, wu):
+    rows = own.shape[0]
+    depth, units = up_near.shape
+    acc = pltpu.VMEM((rows, units), F32)
+    return pl.pallas_call(
+        near_body,
+        in_specs=[VMEM] * 5 + [HBM],
+        out_specs=[VMEM] * 4,
+        out_shape=[acc, acc, pltpu.VMEM((rows, expo.shape[0]), F32), pltpu.VMEM((depth, units), BF16)],
+        input_output_aliases={4: 3},
+        scratch_shapes=[
+            pltpu.VMEM((rows, depth), BF16),
+            pltpu.SemaphoreType.DMA((units // TILE,)),
+        ],
+        cost_estimate=pl.CostEstimate(
+            flops=4 * rows * depth * units, bytes_accessed=2 * depth * units, transcendentals=0
+        ),
+        compiler_params=pltpu.CompilerParams(vmem_limit_bytes=SCOPE),
+        name="near",
+    )(own, mate, expo, wg, up_near, wu)
+
+
+def far_body(
+    own, mate, cross, cross_mate, expo, acc_g, acc_u, limits, up_far, wg, wd, send, keep,
+    left, partial, buf, sem,
 ):
+    del expo
     chip, core = place()
     expert = lax.axis_index("expert")
     rows = own.shape[0]
     width = own.shape[1] - LANES
+    depth = 2 * width
     slots = buf.shape[0]
-    cuts = hid.shape[1] // CUT
-
-    def owner(block):
-        to_chip = chip if block % 2 == 0 else 1 - chip
-        return 2 * to_chip + (1 - core if block < 2 else core)
+    cuts = wd.shape[1] // CUT
 
     def copy(unit):
-        part = wd.at[0, pl.ds(unit % cuts * CUT, CUT), span(owner(unit // cuts), width)]
+        part = wd.at[0, pl.ds(unit * CUT, CUT)]
         return pltpu.make_async_copy(part, buf.at[unit % slots], sem.at[unit % slots])
 
     for unit in range(slots):
         copy(unit).start()
-
-    for to_chip, first, second in ((chip, own, mate), (1 - chip, cross, cross_mate)):
-        left[:, span(2 * to_chip + core, width)] = first[:, :width]
-        left[:, span(2 * to_chip + 1 - core, width)] = second[:, :width]
+    fill_left(left, cross, cross_mate, core, width)
 
     meta = own[:, width:].astype(F32)
     lane = lax.broadcasted_iota(jnp.int32, meta.shape, 1)
@@ -213,68 +291,60 @@
         first = jnp.where(index == expert, logit, first)
         other = jnp.where(routed & (index != expert), logit, other)
     weight = jnp.where(code >= 0.0, 1.0 / (1.0 + jnp.exp(other - first)), 0.0)
-    slots_each = rows // EXPERTS
-    row = lax.broadcasted_iota(jnp.int32, (rows, rows), 0)
-    source = jnp.bitwise_xor(row // slots_each, expert)
-    target = jnp.where(code >= 0.0, (source * slots_each).astype(F32) + code, -1.0)
-    chosen = lax.broadcasted_iota(jnp.int32, (rows, rows), 1).astype(F32) == target
-    table = 448.0 * jnp.exp2(-expo[...].astype(F32))
-    limits[...] = lax.dot_general(
-        chosen.astype(BF16), table.astype(BF16), (((1,), (1,)), ((), ())), preferred_element_type=F32
-    )
-
-    @pl.loop(0, wg.shape[1] // TILE)
-    def _(index):
-        for sub in range(TILE // SUB):
-            columns = span(index * (TILE // SUB) + sub, SUB)
-            gate = jnp.dot(left[...], wg[:, columns], preferred_element_type=F32)
-            up = jnp.dot(left[...], wu[:, columns], preferred_element_type=F32)
-            hid[:, columns] = (gate / (1.0 + jnp.exp(-gate)) * up).astype(BF16)
-
-    unit = 0
+
+    for unit in range(cuts):
+        pieces = []
+        for sub in range(unit * CUT // SUB, (unit + 1) * CUT // SUB):
+            columns = slice(sub * SUB, (sub + 1) * SUB)
+            gate = acc_g[:, columns] + jnp.dot(
+                left[...], wg[span(1 - chip, depth), columns], preferred_element_type=F32
+            )
+            up = acc_u[:, columns] + jnp.dot(
+                left[...], up_far[:, columns], preferred_element_type=F32
+            )
+            pieces.append((gate / (1.0 + jnp.exp(-gate)) * up).astype(BF16))
+        hidden = jnp.concatenate(pieces, axis=1)
+        copy(unit).wait()
+        term = jnp.dot(hidden, buf[unit % slots], preferred_element_type=F32)
+        partial[...] = term if unit == 0 else partial[...] + term
+        if unit + slots < cuts:
+            copy(unit + slots).start()
+
+    blocks = lax.broadcasted_iota(jnp.int32, limits.shape, 1)
     for block in range(4):
-        partial = None
-        for cut in range(cuts):
-            copy(unit).wait()
-            term = jnp.dot(
-                hid[:, cut * CUT : (cut + 1) * CUT], buf[unit % slots], preferred_element_type=F32
-            )
-            partial = term if partial is None else partial + term
-            if unit + slots < 4 * cuts:
-                copy(unit + slots).start()
-            unit += 1
+        to_chip = chip if block % 2 == 0 else 1 - chip
+        owner = 2 * to_chip + (1 - core if block < 2 else core)
+        sums = partial[:, span(owner, width)]
         out = (send, keep)[block // 2]
-        blocks = lax.broadcasted_iota(jnp.int32, limits.shape, 1)
         for piece in range(width // LANES):
             columns = slice(piece * LANES, (piece + 1) * LANES)
-            feature = owner(block) * (width // LANES) + piece
+            feature = owner * (width // LANES) + piece
             bound = jnp.sum(jnp.where(blocks == feature, limits[...], 0.0), axis=1, keepdims=True)
-            coded = jnp.clip(partial[:, columns], -bound, bound).astype(BF16).astype(F32)
+            coded = jnp.clip(sums[:, columns], -bound, bound).astype(BF16).astype(F32)
             out[block % 2, :, columns] = (coded * weight).astype(out.dtype)
 
 
-def main(own, mate, cross, cross_mate, expo, wg, wu, wd):
-    rows, width = own.shape
-    width = width - LANES
-    depth, units = wg.shape
-    return pl.pallas_call(
-        main_body,
-        in_specs=[VMEM] * 7 + [HBM],
+def far(own, mate, cross, cross_mate, expo, acc_g, acc_u, limits, up_far, wg, wd):
+    rows = own.shape[0]
+    depth, units = up_far.shape
+    width = depth // 2
+    return pl.pallas_call(
+        far_body,
+        in_specs=[VMEM] * 10 + [HBM],
         out_specs=[VMEM, VMEM],
         out_shape=[pltpu.VMEM((2, rows, width), BF16), pltpu.VMEM((2, rows, width), F32)],
         scratch_shapes=[
             pltpu.VMEM((rows, depth), BF16),
-            pltpu.VMEM((rows, units), BF16),
-            pltpu.VMEM((rows, expo.shape[0]), F32),
-            pltpu.VMEM((SLOTS, CUT, width), BF16),
+            pltpu.VMEM((rows, wd.shape[2]), F32),
+            pltpu.VMEM((SLOTS, CUT, wd.shape[2]), BF16),
             pltpu.SemaphoreType.DMA((SLOTS,)),
         ],
         cost_estimate=pl.CostEstimate(
-            flops=6 * rows * depth * units, bytes_accessed=6 * depth * units, transcendentals=0
+            flops=8 * rows * depth * units, bytes_accessed=4 * depth * units, transcendentals=0
         ),
         compiler_params=pltpu.CompilerParams(vmem_limit_bytes=SCOPE),
-        name="main",
-    )(own, mate, cross, cross_mate, expo, wg, wu, wd)
+        name="far",
+    )(own, mate, cross, cross_mate, expo, acc_g, acc_u, limits, up_far, wg, wd)
 
 
 def split_body(keep, got, *outs):
@@ -316,22 +386,30 @@
     )(*parts)
 
 
+RETURNS = ((1, 2), (1, 0), (0, 2), (3, 2), (3, 0), (2, 2), (2, 0))
+
+
 def fast(tokens, router_weight, routes, slots, gate_weight, up_weight, down_weight, scale_exponents):
     packed = pack(tokens, router_weight.T, routes.T, slots.T)
-    own = in_vmem(join([packed] + [swap(packed, bits, 0) for bits in (1, 2, 3)]))
+    up_weight = in_hbm(up_weight)
+    wg = in_vmem(gate_weight[0])
+    arrived = [swap(packed, bits, 0) for bits in (1, 2, 3)]
+    packed, up_near = lax.optimization_barrier((packed, fetch(up_weight)))
+    own = in_vmem(join([packed] + arrived))
     mate = in_vmem(swap(own, 0, 1))
-    cross = in_vmem(swap(own, 0, 2))
+    cross = swap(own, 0, 2)
+    expo = in_vmem(scale_exponents[0, 0].T)
+    held = near(own, mate, expo, wg, in_vmem(up_near), up_weight)
+    cross, *held = lax.optimization_barrier((cross, *held))
+    cross = in_vmem(cross)
     cross_mate = in_vmem(swap(cross, 0, 1))
-    send, keep = main(
-        own, mate, cross, cross_mate, in_vmem(scale_exponents[0, 0].T),
-        in_vmem(gate_weight[0]), in_vmem(up_weight[0]), in_hbm(down_weight),
+    send, keep = far(
+        own, mate, cross, cross_mate, expo, *map(in_vmem, held), wg, in_hbm(down_weight)
     )
     blocks = split(in_vmem(keep), in_vmem(swap(send, 0, 1)))
     parts = [blocks[0]]
-    for bits in (3, 2, 1):
-        for chip in (2, 0):
-            parts.append(swap(blocks[(chip // 2) * EXPERTS + bits], bits, chip))
-    parts.append(swap(blocks[EXPERTS], 0, 2))
+    for bits, chip in RETURNS:
+        parts.append(swap(blocks[(chip // 2) * EXPERTS + bits], bits, chip))
     return total(parts)
 
 

time: 54.5 us -> 50.5 us (0.927)
  waiting for transfers between devices: 16.3 us -> 8.67 us
  Pallas kernels: 19.3 us -> 22.8 us
    ppermute x14, waiting for transfers between devices: 16.3 us -> 8.67 us  [swap(): return lax.ppermute(value, JOINT, pairs)]
    pallas_call x1 -> x3, Pallas kernels: 17.4 us -> 20.9 us  [the longest x1 10.6 us: far(): pl.pallas_call(far_body, in_specs=[VMEM] * 10 + [HBM], out_specs=[VMEM, V...]
  transfers between devices with their start and end apart: 14 -> 14, of which waited for: 10 -> 9; matrix products, arithmetic and copies ran while one was open for 0% -> 0% of each run, Pallas kernels for 0% -> 20%
where the time goes in v3:
time: 50.5 us; the launch traced here: 50.4 us
  Pallas kernels  22.8 us (45%)
  starting transfers between devices  18.7 us (37%)
  waiting for transfers between devices  8.67 us (17%)
    ppermute x14, starting transfers between devices, swap(): return lax.ppermute(value, JOINT, pairs)  18.7 us
    pallas_call x1, Pallas kernels, far(): pl.pallas_call(far_body, in_specs=[VMEM] * 10 + [HBM], out_specs=[VMEM, V...  10.6 us
    ppermute x14, waiting for transfers between devices, swap(): return lax.ppermute(value, JOINT, pairs)  8.67 us
    pallas_call x1, Pallas kernels, near(): pl.pallas_call(near_body, in_specs=[VMEM] * 5 + [HBM], out_specs=[VMEM] *...  5.26 us
    pallas_call x1, Pallas kernels, fetch(): pl.pallas_call(fetch_body, in_specs=[HBM], out_specs=VMEM, out_shape=pltp...  5.04 us
    pallas_call x1, Pallas kernels, pack(): pl.pallas_call(pack_body, in_specs=[HBM] * 4, out_specs=VMEM, out_shape=p...  1.11 us
  transfers between devices with their start and end apart: 14, of which 9 were waited for; matrix products, arithmetic and copies ran while one was open for 0% of the time, Pallas kernels for 20%

profile of v3, /device:TPU:0, one launch (start us, length us, event | category | flops | bytes accessed | tf_op | source)
XLA Modules:
  0.0 50.4 jit_solution(6244207707900687561)
XLA Ops:
  0.0 1.1 %pack.1.refs_0_ = bf16[32,896]{1,0:T(8,128)(2,1)S(1)} custom-call(bf16[32,768]{1,0:T(8,128)(2,1)} %tokens.1, f32[4,768]{1,0:T(4,128)} %bitcast.13, s32[2,32]{1,0:T(2,128)} %bitcast.14, s32[2,32]{1,0:T(2,128)} %bitcast.15), custom_call_target="tpu_custom_call" | custom-call | flops 12000000000 | tf_op jit(solution)/shard_map/pack/pallas_call | solution.py:126
  1.2 3.1 %collective-permute-start = (bf16[32,896]{1,0:T(8,128)(2,1)S(1)}, bf16[32,896]{1,0:T(8,128)(2,1)S(1)}, u32[]{:S(2)}, u32[]{:S(2)}) collective-permute-start(bf16[32,896]{1,0:T(8,128)(2,1)S(1)} %pack.1.refs_0_), channel_id=1, source_target_pairs={{0,4},{1,5},{2,6},{3,7},{4,0},{5,1},{6,2},{7,3},{8,12},{9,13},{10,... | collective-permute-start | bytes 172040 | tf_op jit(solution)/shard_map/ppermute | solution.py:78
  4.3 2.6 %collective-permute-start.1 = (bf16[32,896]{1,0:T(8,128)(2,1)S(1)}, bf16[32,896]{1,0:T(8,128)(2,1)S(1)}, u32[]{:S(2)}, u32[]{:S(2)}) collective-permute-start(bf16[32,896]{1,0:T(8,128)(2,1)S(1)} %pack.1.refs_0_), channel_id=1, source_target_pairs={{0,8},{1,9},{2,10},{3,11},{4,12},{5,13},{6,14},{7,15},{8,0},{9,1},... | collective-permute-start | bytes 172040 | tf_op jit(solution)/shard_map/ppermute | solution.py:78
  6.9 5.0 %fetch.1.up_near = bf16[1536,4096]{1,0:T(8,128)(2,1)S(1)} custom-call(bf16[1,3072,4096]{2,1,0:T(8,128)(2,1)} %wu.3), custom_call_target="tpu_custom_call" | custom-call | flops 5000000000 | tf_op jit(solution)/shard_map/fetch/pallas_call | solution.py:190
  11.9 0.9 %collective-permute-done.2.refs_3_ = bf16[32,896]{1,0:T(8,128)(2,1)S(1)} collective-permute-done((bf16[32,896]{1,0:T(8,128)(2,1)S(1)}, bf16[32,896]{1,0:T(8,128)(2,1)S(1)}, u32[]{:S(2)}, u32[]{:S(2)}) %collective-permute-start.2) | collective-permute-done | bytes 57376 | tf_op jit(solution)/shard_map/ppermute | solution.py:78
  12.9 1.6 %collective-permute-start.4 = (bf16[128,896]{1,0:T(8,128)(2,1)S(1)}, bf16[128,896]{1,0:T(8,128)(2,1)S(1)}, u32[]{:S(2)}, u32[]{:S(2)}) collective-permute-start(bf16[128,896]{1,0:T(8,128)(2,1)S(1)} %join.1.own), channel_id=1, source_target_pairs={{0,2},{1,3},{2,0},{3,1},{4,6},{5,7},{6,4},{7,5},{8,10},{9,11},{10,... | collective-permute-start | bytes 688136 | tf_op jit(solution)/shard_map/ppermute | solution.py:78
  14.6 5.3 %near.1 = (f32[128,4096]{1,0:T(8,128)S(1)}, f32[128,4096]{1,0:T(8,128)S(1)}, f32[128,24]{1,0:T(8,128)S(1)}, bf16[1536,4096]{1,0:T(8,128)(2,1)S(1)}) custom-call(bf16[128,896]{1,0:T(8,128)(2,1)S(1)} %join.1.own, bf16[128,896]{1,0:T(8,128)(2,1)S(1)} %collective-permute-done.3.mate, s32[24,128]{1,0:T(8,128)S(1)} %bitcast.11, ...), custom_call_target="tpu_custom_call", output_to_operand_aliasing={{3}: (4, {})} | custom-call | flops 3221225472 | bytes 12582912 | tf_op jit(solution)/shard_map/near/pallas_call | solution.py:240
  19.8 1.1 %collective-permute-done.4.cross = bf16[128,896]{1,0:T(8,128)(2,1)S(1)} collective-permute-done((bf16[128,896]{1,0:T(8,128)(2,1)S(1)}, bf16[128,896]{1,0:T(8,128)(2,1)S(1)}, u32[]{:S(2)}, u32[]{:S(2)}) %collective-permute-start.4) | collective-permute-done | bytes 229408 | tf_op jit(solution)/shard_map/ppermute | solution.py:78
  21.0 1.5 %collective-permute-done.5.cross_mate = bf16[128,896]{1,0:T(8,128)(2,1)S(1)} collective-permute-done((bf16[128,896]{1,0:T(8,128)(2,1)S(1)}, bf16[128,896]{1,0:T(8,128)(2,1)S(1)}, u32[]{:S(2)}, u32[]{:S(2)}) %collective-permute-start.5) | collective-permute-done | bytes 229408 | tf_op jit(solution)/shard_map/ppermute | solution.py:78
  22.4 10.6 %far.1 = (bf16[2,128,768]{2,1,0:T(8,128)(2,1)S(1)}, f32[2,128,768]{2,1,0:T(8,128)S(1)}) custom-call(bf16[128,896]{1,0:T(8,128)(2,1)S(1)} %join.1.own, bf16[128,896]{1,0:T(8,128)(2,1)S(1)} %collective-permute-done.3.mate, bf16[128,896]{1,0:T(8,128)(2,1)S(1)} %collective-permute-done.4.cross, bf16[128,896]{1,0:T(8,128)(2,1)S(1)} %collective-permute-done.5.cross_mate, ...), custom_call_target="tpu_custom_call" | custom-call | flops 6442450944 | bytes 25165824 | tf_op jit(solution)/shard_map/far/pallas_call | solution.py:331
  33.0 0.2 collective-permute-start.6
  33.2 1.6 %collective-permute-done.6.got = bf16[2,128,768]{2,1,0:T(8,128)(2,1)S(1)} collective-permute-done((bf16[2,128,768]{2,1,0:T(8,128)(2,1)S(1)}, bf16[2,128,768]{2,1,0:T(8,128)(2,1)S(1)}, u32[]{:S(2)}, u32[]{:S(2)}) %collective-permute-start.6) | collective-permute-done | bytes 393248 | tf_op jit(solution)/shard_map/ppermute | solution.py:78
  34.9 4.3 %collective-permute-start.10 = (bf16[32,768]{1,0:T(8,128)(2,1)S(1)}, bf16[32,768]{1,0:T(8,128)(2,1)S(1)}, u32[]{:S(2)}, u32[]{:S(2)}) collective-permute-start(bf16[32,768]{1,0:T(8,128)(2,1)S(1)} %get-tuple-element.43), channel_id=1, source_target_pairs={{0,14},{1,15},{2,12},{3,13},{4,10},{5,11},{6,8},{7,9},{8,6},{9,7},... | collective-permute-start | bytes 147464 | tf_op jit(solution)/shard_map/ppermute | solution.py:78
  39.2 0.5 %collective-permute-start.11 = (bf16[32,768]{1,0:T(8,128)(2,1)S(1)}, bf16[32,768]{1,0:T(8,128)(2,1)S(1)}, u32[]{:S(2)}, u32[]{:S(2)}) collective-permute-start(bf16[32,768]{1,0:T(8,128)(2,1)S(1)} %get-tuple-element.44), channel_id=1, source_target_pairs={{0,12},{1,13},{2,14},{3,15},{4,8},{5,9},{6,10},{7,11},{8,4},{9,5},... | collective-permute-start | bytes 147464 | tf_op jit(solution)/shard_map/ppermute | solution.py:78
  39.7 2.9 %collective-permute-start.13 = (bf16[32,768]{1,0:T(8,128)(2,1)S(1)}, bf16[32,768]{1,0:T(8,128)(2,1)S(1)}, u32[]{:S(2)}, u32[]{:S(2)}) collective-permute-start(bf16[32,768]{1,0:T(8,128)(2,1)S(1)} %get-tuple-element.46), channel_id=1, source_target_pairs={{0,8},{1,9},{2,10},{3,11},{4,12},{5,13},{6,14},{7,15},{8,0},{9,1},... | collective-permute-start | bytes 147464 | tf_op jit(solution)/shard_map/ppermute | solution.py:78
  42.6 1.8 %collective-permute-start.7 = (bf16[32,768]{1,0:T(8,128)(2,1)S(1)}, bf16[32,768]{1,0:T(8,128)(2,1)S(1)}, u32[]{:S(2)}, u32[]{:S(2)}) collective-permute-start(bf16[32,768]{1,0:T(8,128)(2,1)S(1)} %get-tuple-element.40), channel_id=1, source_target_pairs={{0,6},{1,7},{2,4},{3,5},{4,2},{5,3},{6,0},{7,1},{8,14},{9,15},{10,... | collective-permute-start | bytes 147464 | tf_op jit(solution)/shard_map/ppermute | solution.py:78
  44.5 1.1 %collective-permute-start.8 = (bf16[32,768]{1,0:T(8,128)(2,1)S(1)}, bf16[32,768]{1,0:T(8,128)(2,1)S(1)}, u32[]{:S(2)}, u32[]{:S(2)}) collective-permute-start(bf16[32,768]{1,0:T(8,128)(2,1)S(1)} %get-tuple-element.41), channel_id=1, source_target_pairs={{0,4},{1,5},{2,6},{3,7},{4,0},{5,1},{6,2},{7,3},{8,12},{9,13},{10,... | collective-permute-start | bytes 147464 | tf_op jit(solution)/shard_map/ppermute | solution.py:78
  45.6 0.5 %collective-permute-start.9 = (bf16[32,768]{1,0:T(8,128)(2,1)S(1)}, bf16[32,768]{1,0:T(8,128)(2,1)S(1)}, u32[]{:S(2)}, u32[]{:S(2)}) collective-permute-start(bf16[32,768]{1,0:T(8,128)(2,1)S(1)} %get-tuple-element.42), channel_id=1, source_target_pairs={{0,2},{1,3},{2,0},{3,1},{4,6},{5,7},{6,4},{7,5},{8,10},{9,11},{10,... | collective-permute-start | bytes 147464 | tf_op jit(solution)/shard_map/ppermute | solution.py:78
  46.1 0.7 %collective-permute-done.12.refs_6_ = bf16[32,768]{1,0:T(8,128)(2,1)S(1)} collective-permute-done((bf16[32,768]{1,0:T(8,128)(2,1)S(1)}, bf16[32,768]{1,0:T(8,128)(2,1)S(1)}, u32[]{:S(2)}, u32[]{:S(2)}) %collective-permute-start.12) | collective-permute-done | bytes 49184 | tf_op jit(solution)/shard_map/ppermute | solution.py:78
  46.8 1.4 %collective-permute-done.13.refs_7_ = bf16[32,768]{1,0:T(8,128)(2,1)S(1)} collective-permute-done((bf16[32,768]{1,0:T(8,128)(2,1)S(1)}, bf16[32,768]{1,0:T(8,128)(2,1)S(1)}, u32[]{:S(2)}, u32[]{:S(2)}) %collective-permute-start.13) | collective-permute-done | bytes 49184 | tf_op jit(solution)/shard_map/ppermute | solution.py:78
  48.2 0.5 %collective-permute-done.7.refs_1_ = bf16[32,768]{1,0:T(8,128)(2,1)S(1)} collective-permute-done((bf16[32,768]{1,0:T(8,128)(2,1)S(1)}, bf16[32,768]{1,0:T(8,128)(2,1)S(1)}, u32[]{:S(2)}, u32[]{:S(2)}) %collective-permute-start.7) | collective-permute-done | bytes 49184 | tf_op jit(solution)/shard_map/ppermute | solution.py:78
  48.7 0.1 collective-permute-done.8.refs_2_
  48.9 0.8 %collective-permute-done.9.refs_3_ = bf16[32,768]{1,0:T(8,128)(2,1)S(1)} collective-permute-done((bf16[32,768]{1,0:T(8,128)(2,1)S(1)}, bf16[32,768]{1,0:T(8,128)(2,1)S(1)}, u32[]{:S(2)}, u32[]{:S(2)}) %collective-permute-start.9) | collective-permute-done | bytes 49184 | tf_op jit(solution)/shard_map/ppermute | solution.py:78
  49.7 0.7 %total.1 = bf16[32,768]{1,0:T(8,128)(2,1)} custom-call(f32[32,768]{1,0:T(8,128)S(1)} %get-tuple-element.39.refs_0_, bf16[32,768]{1,0:T(8,128)(2,1)S(1)} %collective-permute-done.7.refs_1_, bf16[32,768]{1,0:T(8,128)(2,1)S(1)} %collective-permute-done.8.refs_2_, bf16[32,768]{1,0:T(8,128)(2,1)S(1)} %collective-permute-done.9.refs_3_, ...), custom_call_target="tpu_custom_call" | custom-call | tf_op jit(solution)/shard_map/total/pallas_call | solution.py:379
  (26 shorter events, 0.2 us)
Async XLA Ops:
  0.0 14.5 %slice-start = ((s8[25165824]{0:T(1024)(128)(4,1)}), s8[4194304]{0:T(1024)(128)(4,1)S(1)}, s32[]{:S(2)}) async-start(s8[25165824]{0:T(1024)(128)(4,1)} %bitcast.7), calls=%async_computation | async-start | bytes 8388608
  0.0 14.5 %slice-start.1 = ((s8[25165824]{0:T(1024)(128)(4,1)}), s8[4194304]{0:T(1024)(128)(4,1)S(1)}, s32[]{:S(2)}) async-start(s8[25165824]{0:T(1024)(128)(4,1)} %bitcast.7), calls=%async_computation.1 | async-start | bytes 8388608
  0.0 14.5 %slice-start.2 = ((s8[25165824]{0:T(1024)(128)(4,1)}), s8[4194304]{0:T(1024)(128)(4,1)S(1)}, s32[]{:S(2)}) async-start(s8[25165824]{0:T(1024)(128)(4,1)} %bitcast.7), calls=%async_computation.2 | async-start | bytes 8388608
  0.0 14.5 %slice-start.3 = ((s8[25165824]{0:T(1024)(128)(4,1)}), s8[4194304]{0:T(1024)(128)(4,1)S(1)}, s32[]{:S(2)}) async-start(s8[25165824]{0:T(1024)(128)(4,1)} %bitcast.7), calls=%async_computation.3 | async-start | bytes 8388608
  1.1 13.4 %slice-start.4 = ((s8[25165824]{0:T(1024)(128)(4,1)}), s8[4194304]{0:T(1024)(128)(4,1)S(1)}, s32[]{:S(2)}) async-start(s8[25165824]{0:T(1024)(128)(4,1)} %bitcast.7), calls=%async_computation.4 | async-start | bytes 8388608
  1.1 13.4 %slice-start.5 = ((s8[25165824]{0:T(1024)(128)(4,1)}), s8[4194304]{0:T(1024)(128)(4,1)S(1)}, s32[]{:S(2)}) async-start(s8[25165824]{0:T(1024)(128)(4,1)} %bitcast.7), calls=%async_computation.5 | async-start | bytes 8388608
  1.2 13.4 %copy-start = (s32[1,1,128,24]{2,3,1,0:T(8,128)S(1)}, s32[1,1,128,24]{2,3,1,0:T(8,128)}, u32[]{:S(2)}) copy-start(s32[1,1,128,24]{2,3,1,0:T(8,128)} %param.15) | copy-start | bytes 36868
  1.2 10.7 %collective-permute-start = (bf16[32,896]{1,0:T(8,128)(2,1)S(1)}, bf16[32,896]{1,0:T(8,128)(2,1)S(1)}, u32[]{:S(2)}, u32[]{:S(2)}) collective-permute-start(bf16[32,896]{1,0:T(8,128)(2,1)S(1)} %pack.1.refs_0_), channel_id=1, source_target_pairs={{0,4},{1,5},{2,6},{3,7},{4,0},{5,1},{6,2},{7,3},{8,12},{9,13},{10,... | collective-permute-start | bytes 172040 | tf_op jit(solution)/shard_map/ppermute | solution.py:78
  4.3 7.6 %collective-permute-start.1 = (bf16[32,896]{1,0:T(8,128)(2,1)S(1)}, bf16[32,896]{1,0:T(8,128)(2,1)S(1)}, u32[]{:S(2)}, u32[]{:S(2)}) collective-permute-start(bf16[32,896]{1,0:T(8,128)(2,1)S(1)} %pack.1.refs_0_), channel_id=1, source_target_pairs={{0,8},{1,9},{2,10},{3,11},{4,12},{5,13},{6,14},{7,15},{8,0},{9,1},... | collective-permute-start | bytes 172040 | tf_op jit(solution)/shard_map/ppermute | solution.py:78
  6.9 6.0 %collective-permute-start.2 = (bf16[32,896]{1,0:T(8,128)(2,1)S(1)}, bf16[32,896]{1,0:T(8,128)(2,1)S(1)}, u32[]{:S(2)}, u32[]{:S(2)}) collective-permute-start(bf16[32,896]{1,0:T(8,128)(2,1)S(1)} %pack.1.refs_0_), channel_id=1, source_target_pairs={{0,12},{1,13},{2,14},{3,15},{4,8},{5,9},{6,10},{7,11},{8,4},{9,5},... | collective-permute-start | bytes 172040 | tf_op jit(solution)/shard_map/ppermute | solution.py:78
  12.9 1.6 %collective-permute-start.3 = (bf16[128,896]{1,0:T(8,128)(2,1)S(1)}, bf16[128,896]{1,0:T(8,128)(2,1)S(1)}, u32[]{:S(2)}, u32[]{:S(2)}) collective-permute-start(bf16[128,896]{1,0:T(8,128)(2,1)S(1)} %join.1.own), channel_id=1, source_target_pairs={{0,1},{1,0},{2,3},{3,2},{4,5},{5,4},{6,7},{7,6},{8,9},{9,8},{10,11... | collective-permute-start | bytes 688136 | tf_op jit(solution)/shard_map/ppermute | solution.py:78
  12.9 8.0 %collective-permute-start.4 = (bf16[128,896]{1,0:T(8,128)(2,1)S(1)}, bf16[128,896]{1,0:T(8,128)(2,1)S(1)}, u32[]{:S(2)}, u32[]{:S(2)}) collective-permute-start(bf16[128,896]{1,0:T(8,128)(2,1)S(1)} %join.1.own), channel_id=1, source_target_pairs={{0,2},{1,3},{2,0},{3,1},{4,6},{5,7},{6,4},{7,5},{8,10},{9,11},{10,... | collective-permute-start | bytes 688136 | tf_op jit(solution)/shard_map/ppermute | solution.py:78
  21.0 1.5 %collective-permute-start.5 = (bf16[128,896]{1,0:T(8,128)(2,1)S(1)}, bf16[128,896]{1,0:T(8,128)(2,1)S(1)}, u32[]{:S(2)}, u32[]{:S(2)}) collective-permute-start(bf16[128,896]{1,0:T(8,128)(2,1)S(1)} %collective-permute-done.4.cross), channel_id=1, source_target_pairs={{0,1},{1,0},{2,3},{3,2},{4,5},{5,4},{6,7},{7,6},{8,9},{9,8},{10,11... | collective-permute-start | bytes 688136 | tf_op jit(solution)/shard_map/ppermute | solution.py:78
  33.0 1.8 %collective-permute-start.6 = (bf16[2,128,768]{2,1,0:T(8,128)(2,1)S(1)}, bf16[2,128,768]{2,1,0:T(8,128)(2,1)S(1)}, u32[]{:S(2)}, u32[]{:S(2)}) collective-permute-start(bf16[2,128,768]{2,1,0:T(8,128)(2,1)S(1)} %get-tuple-element.38), channel_id=1, source_target_pairs={{0,1},{1,0},{2,3},{3,2},{4,5},{5,4},{6,7},{7,6},{8,9},{9,8},{10,11... | collective-permute-start | bytes 1179656 | tf_op jit(solution)/shard_map/ppermute | solution.py:78
  34.9 9.6 %collective-permute-start.10 = (bf16[32,768]{1,0:T(8,128)(2,1)S(1)}, bf16[32,768]{1,0:T(8,128)(2,1)S(1)}, u32[]{:S(2)}, u32[]{:S(2)}) collective-permute-start(bf16[32,768]{1,0:T(8,128)(2,1)S(1)} %get-tuple-element.43), channel_id=1, source_target_pairs={{0,14},{1,15},{2,12},{3,13},{4,10},{5,11},{6,8},{7,9},{8,6},{9,7},... | collective-permute-start | bytes 147464 | tf_op jit(solution)/shard_map/ppermute | solution.py:78
  39.2 6.4 %collective-permute-start.11 = (bf16[32,768]{1,0:T(8,128)(2,1)S(1)}, bf16[32,768]{1,0:T(8,128)(2,1)S(1)}, u32[]{:S(2)}, u32[]{:S(2)}) collective-permute-start(bf16[32,768]{1,0:T(8,128)(2,1)S(1)} %get-tuple-element.44), channel_id=1, source_target_pairs={{0,12},{1,13},{2,14},{3,15},{4,8},{5,9},{6,10},{7,11},{8,4},{9,5},... | collective-permute-start | bytes 147464 | tf_op jit(solution)/shard_map/ppermute | solution.py:78
  39.7 7.1 %collective-permute-start.12 = (bf16[32,768]{1,0:T(8,128)(2,1)S(1)}, bf16[32,768]{1,0:T(8,128)(2,1)S(1)}, u32[]{:S(2)}, u32[]{:S(2)}) collective-permute-start(bf16[32,768]{1,0:T(8,128)(2,1)S(1)} %get-tuple-element.45), channel_id=1, source_target_pairs={{0,10},{1,11},{2,8},{3,9},{4,14},{5,15},{6,12},{7,13},{8,2},{9,3},... | collective-permute-start | bytes 147464 | tf_op jit(solution)/shard_map/ppermute | solution.py:78
  39.7 8.5 %collective-permute-start.13 = (bf16[32,768]{1,0:T(8,128)(2,1)S(1)}, bf16[32,768]{1,0:T(8,128)(2,1)S(1)}, u32[]{:S(2)}, u32[]{:S(2)}) collective-permute-start(bf16[32,768]{1,0:T(8,128)(2,1)S(1)} %get-tuple-element.46), channel_id=1, source_target_pairs={{0,8},{1,9},{2,10},{3,11},{4,12},{5,13},{6,14},{7,15},{8,0},{9,1},... | collective-permute-start | bytes 147464 | tf_op jit(solution)/shard_map/ppermute | solution.py:78
  42.6 6.1 %collective-permute-start.7 = (bf16[32,768]{1,0:T(8,128)(2,1)S(1)}, bf16[32,768]{1,0:T(8,128)(2,1)S(1)}, u32[]{:S(2)}, u32[]{:S(2)}) collective-permute-start(bf16[32,768]{1,0:T(8,128)(2,1)S(1)} %get-tuple-element.40), channel_id=1, source_target_pairs={{0,6},{1,7},{2,4},{3,5},{4,2},{5,3},{6,0},{7,1},{8,14},{9,15},{10,... | collective-permute-start | bytes 147464 | tf_op jit(solution)/shard_map/ppermute | solution.py:78
  44.5 4.4 %collective-permute-start.8 = (bf16[32,768]{1,0:T(8,128)(2,1)S(1)}, bf16[32,768]{1,0:T(8,128)(2,1)S(1)}, u32[]{:S(2)}, u32[]{:S(2)}) collective-permute-start(bf16[32,768]{1,0:T(8,128)(2,1)S(1)} %get-tuple-element.41), channel_id=1, source_target_pairs={{0,4},{1,5},{2,6},{3,7},{4,0},{5,1},{6,2},{7,3},{8,12},{9,13},{10,... | collective-permute-start | bytes 147464 | tf_op jit(solution)/shard_map/ppermute | solution.py:78
  45.6 4.1 %collective-permute-start.9 = (bf16[32,768]{1,0:T(8,128)(2,1)S(1)}, bf16[32,768]{1,0:T(8,128)(2,1)S(1)}, u32[]{:S(2)}, u32[]{:S(2)}) collective-permute-start(bf16[32,768]{1,0:T(8,128)(2,1)S(1)} %get-tuple-element.42), channel_id=1, source_target_pairs={{0,2},{1,3},{2,0},{3,1},{4,6},{5,7},{6,4},{7,5},{8,10},{9,11},{10,... | collective-permute-start | bytes 147464 | tf_op jit(solution)/shard_map/ppermute | solution.py:78

commit v4 on v3

--- a/solution.py
+++ b/solution.py
@@ -176,7 +176,7 @@
 SCOPE = 18 * MIB
 SLOTS = 4
 CUT = 512
-SUB = 256
+SUB = 512
 
 
 def fetch_body(wu, out, sem):

time: 50.5 us -> 50 us (0.990)
  Pallas kernels: 22.8 us -> 22.2 us
    pallas_call x1, Pallas kernels: 10.6 us -> 10 us  [far(): pl.pallas_call(far_body, in_specs=[VMEM] * 10 + [HBM], out_specs=[VMEM, V...]
  transfers between devices with their start and end apart: 14 -> 14, of which waited for: 9 -> 9; matrix products, arithmetic and copies ran while one was open for 0% -> 0% of each run, Pallas kernels for 20% -> 21%
where the time goes in v4:
time: 50 us; the launch traced here: 49.8 us
  Pallas kernels  22.2 us (44%)
  starting transfers between devices  18.7 us (37%)
  waiting for transfers between devices  8.66 us (17%)
    ppermute x14, starting transfers between devices, swap(): return lax.ppermute(value, JOINT, pairs)  18.7 us
    pallas_call x1, Pallas kernels, far(): pl.pallas_call(far_body, in_specs=[VMEM] * 10 + [HBM], out_specs=[VMEM, V...  10 us
    ppermute x14, waiting for transfers between devices, swap(): return lax.ppermute(value, JOINT, pairs)  8.66 us
    pallas_call x1, Pallas kernels, near(): pl.pallas_call(near_body, in_specs=[VMEM] * 5 + [HBM], out_specs=[VMEM] *...  5.26 us
    pallas_call x1, Pallas kernels, fetch(): pl.pallas_call(fetch_body, in_specs=[HBM], out_specs=VMEM, out_shape=pltp...  5.04 us
    pallas_call x1, Pallas kernels, pack(): pl.pallas_call(pack_body, in_specs=[HBM] * 4, out_specs=VMEM, out_shape=p...  1.11 us
  transfers between devices with their start and end apart: 14, of which 9 were waited for; matrix products, arithmetic and copies ran while one was open for 0% of the time, Pallas kernels for 21%

profile of v4, /device:TPU:0, one launch (start us, length us, event | category | flops | bytes accessed | tf_op | source)
XLA Modules:
  0.0 49.8 jit_solution(10085541931076299855)
XLA Ops:
  0.0 1.1 %pack.1.refs_0_ = bf16[32,896]{1,0:T(8,128)(2,1)S(1)} custom-call(bf16[32,768]{1,0:T(8,128)(2,1)} %tokens.1, f32[4,768]{1,0:T(4,128)} %bitcast.13, s32[2,32]{1,0:T(2,128)} %bitcast.14, s32[2,32]{1,0:T(2,128)} %bitcast.15), custom_call_target="tpu_custom_call" | custom-call | flops 12000000000 | tf_op jit(solution)/shard_map/pack/pallas_call | solution.py:126
  1.2 3.1 %collective-permute-start = (bf16[32,896]{1,0:T(8,128)(2,1)S(1)}, bf16[32,896]{1,0:T(8,128)(2,1)S(1)}, u32[]{:S(2)}, u32[]{:S(2)}) collective-permute-start(bf16[32,896]{1,0:T(8,128)(2,1)S(1)} %pack.1.refs_0_), channel_id=1, source_target_pairs={{0,4},{1,5},{2,6},{3,7},{4,0},{5,1},{6,2},{7,3},{8,12},{9,13},{10,... | collective-permute-start | bytes 172040 | tf_op jit(solution)/shard_map/ppermute | solution.py:78
  4.3 2.6 %collective-permute-start.1 = (bf16[32,896]{1,0:T(8,128)(2,1)S(1)}, bf16[32,896]{1,0:T(8,128)(2,1)S(1)}, u32[]{:S(2)}, u32[]{:S(2)}) collective-permute-start(bf16[32,896]{1,0:T(8,128)(2,1)S(1)} %pack.1.refs_0_), channel_id=1, source_target_pairs={{0,8},{1,9},{2,10},{3,11},{4,12},{5,13},{6,14},{7,15},{8,0},{9,1},... | collective-permute-start | bytes 172040 | tf_op jit(solution)/shard_map/ppermute | solution.py:78
  6.9 5.0 %fetch.1.up_near = bf16[1536,4096]{1,0:T(8,128)(2,1)S(1)} custom-call(bf16[1,3072,4096]{2,1,0:T(8,128)(2,1)} %wu.3), custom_call_target="tpu_custom_call" | custom-call | flops 5000000000 | tf_op jit(solution)/shard_map/fetch/pallas_call | solution.py:190
  11.9 0.9 %collective-permute-done.2.refs_3_ = bf16[32,896]{1,0:T(8,128)(2,1)S(1)} collective-permute-done((bf16[32,896]{1,0:T(8,128)(2,1)S(1)}, bf16[32,896]{1,0:T(8,128)(2,1)S(1)}, u32[]{:S(2)}, u32[]{:S(2)}) %collective-permute-start.2) | collective-permute-done | bytes 57376 | tf_op jit(solution)/shard_map/ppermute | solution.py:78
  12.9 1.6 %collective-permute-start.4 = (bf16[128,896]{1,0:T(8,128)(2,1)S(1)}, bf16[128,896]{1,0:T(8,128)(2,1)S(1)}, u32[]{:S(2)}, u32[]{:S(2)}) collective-permute-start(bf16[128,896]{1,0:T(8,128)(2,1)S(1)} %join.1.own), channel_id=1, source_target_pairs={{0,2},{1,3},{2,0},{3,1},{4,6},{5,7},{6,4},{7,5},{8,10},{9,11},{10,... | collective-permute-start | bytes 688136 | tf_op jit(solution)/shard_map/ppermute | solution.py:78
  14.6 5.3 %near.1 = (f32[128,4096]{1,0:T(8,128)S(1)}, f32[128,4096]{1,0:T(8,128)S(1)}, f32[128,24]{1,0:T(8,128)S(1)}, bf16[1536,4096]{1,0:T(8,128)(2,1)S(1)}) custom-call(bf16[128,896]{1,0:T(8,128)(2,1)S(1)} %join.1.own, bf16[128,896]{1,0:T(8,128)(2,1)S(1)} %collective-permute-done.3.mate, s32[24,128]{1,0:T(8,128)S(1)} %bitcast.11, ...), custom_call_target="tpu_custom_call", output_to_operand_aliasing={{3}: (4, {})} | custom-call | flops 3221225472 | bytes 12582912 | tf_op jit(solution)/shard_map/near/pallas_call | solution.py:240
  19.8 1.1 %collective-permute-done.4.cross = bf16[128,896]{1,0:T(8,128)(2,1)S(1)} collective-permute-done((bf16[128,896]{1,0:T(8,128)(2,1)S(1)}, bf16[128,896]{1,0:T(8,128)(2,1)S(1)}, u32[]{:S(2)}, u32[]{:S(2)}) %collective-permute-start.4) | collective-permute-done | bytes 229408 | tf_op jit(solution)/shard_map/ppermute | solution.py:78
  21.0 1.5 %collective-permute-done.5.cross_mate = bf16[128,896]{1,0:T(8,128)(2,1)S(1)} collective-permute-done((bf16[128,896]{1,0:T(8,128)(2,1)S(1)}, bf16[128,896]{1,0:T(8,128)(2,1)S(1)}, u32[]{:S(2)}, u32[]{:S(2)}) %collective-permute-start.5) | collective-permute-done | bytes 229408 | tf_op jit(solution)/shard_map/ppermute | solution.py:78
  22.4 10.0 %far.1 = (bf16[2,128,768]{2,1,0:T(8,128)(2,1)S(1)}, f32[2,128,768]{2,1,0:T(8,128)S(1)}) custom-call(bf16[128,896]{1,0:T(8,128)(2,1)S(1)} %join.1.own, bf16[128,896]{1,0:T(8,128)(2,1)S(1)} %collective-permute-done.3.mate, bf16[128,896]{1,0:T(8,128)(2,1)S(1)} %collective-permute-done.4.cross, bf16[128,896]{1,0:T(8,128)(2,1)S(1)} %collective-permute-done.5.cross_mate, ...), custom_call_target="tpu_custom_call" | custom-call | flops 6442450944 | bytes 25165824 | tf_op jit(solution)/shard_map/far/pallas_call | solution.py:331
  32.5 0.2 collective-permute-start.6
  32.7 1.6 %collective-permute-done.6.got = bf16[2,128,768]{2,1,0:T(8,128)(2,1)S(1)} collective-permute-done((bf16[2,128,768]{2,1,0:T(8,128)(2,1)S(1)}, bf16[2,128,768]{2,1,0:T(8,128)(2,1)S(1)}, u32[]{:S(2)}, u32[]{:S(2)}) %collective-permute-start.6) | collective-permute-done | bytes 393248 | tf_op jit(solution)/shard_map/ppermute | solution.py:78
  34.4 4.3 %collective-permute-start.10 = (bf16[32,768]{1,0:T(8,128)(2,1)S(1)}, bf16[32,768]{1,0:T(8,128)(2,1)S(1)}, u32[]{:S(2)}, u32[]{:S(2)}) collective-permute-start(bf16[32,768]{1,0:T(8,128)(2,1)S(1)} %get-tuple-element.43), channel_id=1, source_target_pairs={{0,14},{1,15},{2,12},{3,13},{4,10},{5,11},{6,8},{7,9},{8,6},{9,7},... | collective-permute-start | bytes 147464 | tf_op jit(solution)/shard_map/ppermute | solution.py:78
  38.7 0.5 %collective-permute-start.11 = (bf16[32,768]{1,0:T(8,128)(2,1)S(1)}, bf16[32,768]{1,0:T(8,128)(2,1)S(1)}, u32[]{:S(2)}, u32[]{:S(2)}) collective-permute-start(bf16[32,768]{1,0:T(8,128)(2,1)S(1)} %get-tuple-element.44), channel_id=1, source_target_pairs={{0,12},{1,13},{2,14},{3,15},{4,8},{5,9},{6,10},{7,11},{8,4},{9,5},... | collective-permute-start | bytes 147464 | tf_op jit(solution)/shard_map/ppermute | solution.py:78
  39.2 2.9 %collective-permute-start.13 = (bf16[32,768]{1,0:T(8,128)(2,1)S(1)}, bf16[32,768]{1,0:T(8,128)(2,1)S(1)}, u32[]{:S(2)}, u32[]{:S(2)}) collective-permute-start(bf16[32,768]{1,0:T(8,128)(2,1)S(1)} %get-tuple-element.46), channel_id=1, source_target_pairs={{0,8},{1,9},{2,10},{3,11},{4,12},{5,13},{6,14},{7,15},{8,0},{9,1},... | collective-permute-start | bytes 147464 | tf_op jit(solution)/shard_map/ppermute | solution.py:78
  42.1 1.9 %collective-permute-start.7 = (bf16[32,768]{1,0:T(8,128)(2,1)S(1)}, bf16[32,768]{1,0:T(8,128)(2,1)S(1)}, u32[]{:S(2)}, u32[]{:S(2)}) collective-permute-start(bf16[32,768]{1,0:T(8,128)(2,1)S(1)} %get-tuple-element.40), channel_id=1, source_target_pairs={{0,6},{1,7},{2,4},{3,5},{4,2},{5,3},{6,0},{7,1},{8,14},{9,15},{10,... | collective-permute-start | bytes 147464 | tf_op jit(solution)/shard_map/ppermute | solution.py:78
  44.0 1.1 %collective-permute-start.8 = (bf16[32,768]{1,0:T(8,128)(2,1)S(1)}, bf16[32,768]{1,0:T(8,128)(2,1)S(1)}, u32[]{:S(2)}, u32[]{:S(2)}) collective-permute-start(bf16[32,768]{1,0:T(8,128)(2,1)S(1)} %get-tuple-element.41), channel_id=1, source_target_pairs={{0,4},{1,5},{2,6},{3,7},{4,0},{5,1},{6,2},{7,3},{8,12},{9,13},{10,... | collective-permute-start | bytes 147464 | tf_op jit(solution)/shard_map/ppermute | solution.py:78
  45.1 0.5 %collective-permute-start.9 = (bf16[32,768]{1,0:T(8,128)(2,1)S(1)}, bf16[32,768]{1,0:T(8,128)(2,1)S(1)}, u32[]{:S(2)}, u32[]{:S(2)}) collective-permute-start(bf16[32,768]{1,0:T(8,128)(2,1)S(1)} %get-tuple-element.42), channel_id=1, source_target_pairs={{0,2},{1,3},{2,0},{3,1},{4,6},{5,7},{6,4},{7,5},{8,10},{9,11},{10,... | collective-permute-start | bytes 147464 | tf_op jit(solution)/shard_map/ppermute | solution.py:78
  45.6 0.7 %collective-permute-done.12.refs_6_ = bf16[32,768]{1,0:T(8,128)(2,1)S(1)} collective-permute-done((bf16[32,768]{1,0:T(8,128)(2,1)S(1)}, bf16[32,768]{1,0:T(8,128)(2,1)S(1)}, u32[]{:S(2)}, u32[]{:S(2)}) %collective-permute-start.12) | collective-permute-done | bytes 49184 | tf_op jit(solution)/shard_map/ppermute | solution.py:78
  46.3 1.3 %collective-permute-done.13.refs_7_ = bf16[32,768]{1,0:T(8,128)(2,1)S(1)} collective-permute-done((bf16[32,768]{1,0:T(8,128)(2,1)S(1)}, bf16[32,768]{1,0:T(8,128)(2,1)S(1)}, u32[]{:S(2)}, u32[]{:S(2)}) %collective-permute-start.13) | collective-permute-done | bytes 49184 | tf_op jit(solution)/shard_map/ppermute | solution.py:78
  47.6 0.6 %collective-permute-done.7.refs_1_ = bf16[32,768]{1,0:T(8,128)(2,1)S(1)} collective-permute-done((bf16[32,768]{1,0:T(8,128)(2,1)S(1)}, bf16[32,768]{1,0:T(8,128)(2,1)S(1)}, u32[]{:S(2)}, u32[]{:S(2)}) %collective-permute-start.7) | collective-permute-done | bytes 49184 | tf_op jit(solution)/shard_map/ppermute | solution.py:78
  48.2 0.2 collective-permute-done.8.refs_2_
  48.4 0.8 %collective-permute-done.9.refs_3_ = bf16[32,768]{1,0:T(8,128)(2,1)S(1)} collective-permute-done((bf16[32,768]{1,0:T(8,128)(2,1)S(1)}, bf16[32,768]{1,0:T(8,128)(2,1)S(1)}, u32[]{:S(2)}, u32[]{:S(2)}) %collective-permute-start.9) | collective-permute-done | bytes 49184 | tf_op jit(solution)/shard_map/ppermute | solution.py:78
  49.2 0.7 %total.1 = bf16[32,768]{1,0:T(8,128)(2,1)} custom-call(f32[32,768]{1,0:T(8,128)S(1)} %get-tuple-element.39.refs_0_, bf16[32,768]{1,0:T(8,128)(2,1)S(1)} %collective-permute-done.7.refs_1_, bf16[32,768]{1,0:T(8,128)(2,1)S(1)} %collective-permute-done.8.refs_2_, bf16[32,768]{1,0:T(8,128)(2,1)S(1)} %collective-permute-done.9.refs_3_, ...), custom_call_target="tpu_custom_call" | custom-call | tf_op jit(solution)/shard_map/total/pallas_call | solution.py:379
  (26 shorter events, 0.2 us)
Async XLA Ops:
  0.0 14.5 %slice-start = ((s8[25165824]{0:T(1024)(128)(4,1)}), s8[4194304]{0:T(1024)(128)(4,1)S(1)}, s32[]{:S(2)}) async-start(s8[25165824]{0:T(1024)(128)(4,1)} %bitcast.7), calls=%async_computation | async-start | bytes 8388608
  0.0 14.5 %slice-start.1 = ((s8[25165824]{0:T(1024)(128)(4,1)}), s8[4194304]{0:T(1024)(128)(4,1)S(1)}, s32[]{:S(2)}) async-start(s8[25165824]{0:T(1024)(128)(4,1)} %bitcast.7), calls=%async_computation.1 | async-start | bytes 8388608
  0.0 14.5 %slice-start.2 = ((s8[25165824]{0:T(1024)(128)(4,1)}), s8[4194304]{0:T(1024)(128)(4,1)S(1)}, s32[]{:S(2)}) async-start(s8[25165824]{0:T(1024)(128)(4,1)} %bitcast.7), calls=%async_computation.2 | async-start | bytes 8388608
  0.0 14.5 %slice-start.3 = ((s8[25165824]{0:T(1024)(128)(4,1)}), s8[4194304]{0:T(1024)(128)(4,1)S(1)}, s32[]{:S(2)}) async-start(s8[25165824]{0:T(1024)(128)(4,1)} %bitcast.7), calls=%async_computation.3 | async-start | bytes 8388608
  1.1 13.4 %slice-start.4 = ((s8[25165824]{0:T(1024)(128)(4,1)}), s8[4194304]{0:T(1024)(128)(4,1)S(1)}, s32[]{:S(2)}) async-start(s8[25165824]{0:T(1024)(128)(4,1)} %bitcast.7), calls=%async_computation.4 | async-start | bytes 8388608
  1.1 13.4 %slice-start.5 = ((s8[25165824]{0:T(1024)(128)(4,1)}), s8[4194304]{0:T(1024)(128)(4,1)S(1)}, s32[]{:S(2)}) async-start(s8[25165824]{0:T(1024)(128)(4,1)} %bitcast.7), calls=%async_computation.5 | async-start | bytes 8388608
  1.2 13.4 %copy-start = (s32[1,1,128,24]{2,3,1,0:T(8,128)S(1)}, s32[1,1,128,24]{2,3,1,0:T(8,128)}, u32[]{:S(2)}) copy-start(s32[1,1,128,24]{2,3,1,0:T(8,128)} %param.15) | copy-start | bytes 36868
  1.2 10.7 %collective-permute-start = (bf16[32,896]{1,0:T(8,128)(2,1)S(1)}, bf16[32,896]{1,0:T(8,128)(2,1)S(1)}, u32[]{:S(2)}, u32[]{:S(2)}) collective-permute-start(bf16[32,896]{1,0:T(8,128)(2,1)S(1)} %pack.1.refs_0_), channel_id=1, source_target_pairs={{0,4},{1,5},{2,6},{3,7},{4,0},{5,1},{6,2},{7,3},{8,12},{9,13},{10,... | collective-permute-start | bytes 172040 | tf_op jit(solution)/shard_map/ppermute | solution.py:78
  4.3 7.6 %collective-permute-start.1 = (bf16[32,896]{1,0:T(8,128)(2,1)S(1)}, bf16[32,896]{1,0:T(8,128)(2,1)S(1)}, u32[]{:S(2)}, u32[]{:S(2)}) collective-permute-start(bf16[32,896]{1,0:T(8,128)(2,1)S(1)} %pack.1.refs_0_), channel_id=1, source_target_pairs={{0,8},{1,9},{2,10},{3,11},{4,12},{5,13},{6,14},{7,15},{8,0},{9,1},... | collective-permute-start | bytes 172040 | tf_op jit(solution)/shard_map/ppermute | solution.py:78
  6.9 6.0 %collective-permute-start.2 = (bf16[32,896]{1,0:T(8,128)(2,1)S(1)}, bf16[32,896]{1,0:T(8,128)(2,1)S(1)}, u32[]{:S(2)}, u32[]{:S(2)}) collective-permute-start(bf16[32,896]{1,0:T(8,128)(2,1)S(1)} %pack.1.refs_0_), channel_id=1, source_target_pairs={{0,12},{1,13},{2,14},{3,15},{4,8},{5,9},{6,10},{7,11},{8,4},{9,5},... | collective-permute-start | bytes 172040 | tf_op jit(solution)/shard_map/ppermute | solution.py:78
  12.9 1.6 %collective-permute-start.3 = (bf16[128,896]{1,0:T(8,128)(2,1)S(1)}, bf16[128,896]{1,0:T(8,128)(2,1)S(1)}, u32[]{:S(2)}, u32[]{:S(2)}) collective-permute-start(bf16[128,896]{1,0:T(8,128)(2,1)S(1)} %join.1.own), channel_id=1, source_target_pairs={{0,1},{1,0},{2,3},{3,2},{4,5},{5,4},{6,7},{7,6},{8,9},{9,8},{10,11... | collective-permute-start | bytes 688136 | tf_op jit(solution)/shard_map/ppermute | solution.py:78
  12.9 8.0 %collective-permute-start.4 = (bf16[128,896]{1,0:T(8,128)(2,1)S(1)}, bf16[128,896]{1,0:T(8,128)(2,1)S(1)}, u32[]{:S(2)}, u32[]{:S(2)}) collective-permute-start(bf16[128,896]{1,0:T(8,128)(2,1)S(1)} %join.1.own), channel_id=1, source_target_pairs={{0,2},{1,3},{2,0},{3,1},{4,6},{5,7},{6,4},{7,5},{8,10},{9,11},{10,... | collective-permute-start | bytes 688136 | tf_op jit(solution)/shard_map/ppermute | solution.py:78
  21.0 1.5 %collective-permute-start.5 = (bf16[128,896]{1,0:T(8,128)(2,1)S(1)}, bf16[128,896]{1,0:T(8,128)(2,1)S(1)}, u32[]{:S(2)}, u32[]{:S(2)}) collective-permute-start(bf16[128,896]{1,0:T(8,128)(2,1)S(1)} %collective-permute-done.4.cross), channel_id=1, source_target_pairs={{0,1},{1,0},{2,3},{3,2},{4,5},{5,4},{6,7},{7,6},{8,9},{9,8},{10,11... | collective-permute-start | bytes 688136 | tf_op jit(solution)/shard_map/ppermute | solution.py:78
  32.5 1.8 %collective-permute-start.6 = (bf16[2,128,768]{2,1,0:T(8,128)(2,1)S(1)}, bf16[2,128,768]{2,1,0:T(8,128)(2,1)S(1)}, u32[]{:S(2)}, u32[]{:S(2)}) collective-permute-start(bf16[2,128,768]{2,1,0:T(8,128)(2,1)S(1)} %get-tuple-element.38), channel_id=1, source_target_pairs={{0,1},{1,0},{2,3},{3,2},{4,5},{5,4},{6,7},{7,6},{8,9},{9,8},{10,11... | collective-permute-start | bytes 1179656 | tf_op jit(solution)/shard_map/ppermute | solution.py:78
  34.4 9.6 %collective-permute-start.10 = (bf16[32,768]{1,0:T(8,128)(2,1)S(1)}, bf16[32,768]{1,0:T(8,128)(2,1)S(1)}, u32[]{:S(2)}, u32[]{:S(2)}) collective-permute-start(bf16[32,768]{1,0:T(8,128)(2,1)S(1)} %get-tuple-element.43), channel_id=1, source_target_pairs={{0,14},{1,15},{2,12},{3,13},{4,10},{5,11},{6,8},{7,9},{8,6},{9,7},... | collective-permute-start | bytes 147464 | tf_op jit(solution)/shard_map/ppermute | solution.py:78
  38.7 6.4 %collective-permute-start.11 = (bf16[32,768]{1,0:T(8,128)(2,1)S(1)}, bf16[32,768]{1,0:T(8,128)(2,1)S(1)}, u32[]{:S(2)}, u32[]{:S(2)}) collective-permute-start(bf16[32,768]{1,0:T(8,128)(2,1)S(1)} %get-tuple-element.44), channel_id=1, source_target_pairs={{0,12},{1,13},{2,14},{3,15},{4,8},{5,9},{6,10},{7,11},{8,4},{9,5},... | collective-permute-start | bytes 147464 | tf_op jit(solution)/shard_map/ppermute | solution.py:78
  39.2 7.0 %collective-permute-start.12 = (bf16[32,768]{1,0:T(8,128)(2,1)S(1)}, bf16[32,768]{1,0:T(8,128)(2,1)S(1)}, u32[]{:S(2)}, u32[]{:S(2)}) collective-permute-start(bf16[32,768]{1,0:T(8,128)(2,1)S(1)} %get-tuple-element.45), channel_id=1, source_target_pairs={{0,10},{1,11},{2,8},{3,9},{4,14},{5,15},{6,12},{7,13},{8,2},{9,3},... | collective-permute-start | bytes 147464 | tf_op jit(solution)/shard_map/ppermute | solution.py:78
  39.2 8.4 %collective-permute-start.13 = (bf16[32,768]{1,0:T(8,128)(2,1)S(1)}, bf16[32,768]{1,0:T(8,128)(2,1)S(1)}, u32[]{:S(2)}, u32[]{:S(2)}) collective-permute-start(bf16[32,768]{1,0:T(8,128)(2,1)S(1)} %get-tuple-element.46), channel_id=1, source_target_pairs={{0,8},{1,9},{2,10},{3,11},{4,12},{5,13},{6,14},{7,15},{8,0},{9,1},... | collective-permute-start | bytes 147464 | tf_op jit(solution)/shard_map/ppermute | solution.py:78
  42.1 6.1 %collective-permute-start.7 = (bf16[32,768]{1,0:T(8,128)(2,1)S(1)}, bf16[32,768]{1,0:T(8,128)(2,1)S(1)}, u32[]{:S(2)}, u32[]{:S(2)}) collective-permute-start(bf16[32,768]{1,0:T(8,128)(2,1)S(1)} %get-tuple-element.40), channel_id=1, source_target_pairs={{0,6},{1,7},{2,4},{3,5},{4,2},{5,3},{6,0},{7,1},{8,14},{9,15},{10,... | collective-permute-start | bytes 147464 | tf_op jit(solution)/shard_map/ppermute | solution.py:78
  44.0 4.4 %collective-permute-start.8 = (bf16[32,768]{1,0:T(8,128)(2,1)S(1)}, bf16[32,768]{1,0:T(8,128)(2,1)S(1)}, u32[]{:S(2)}, u32[]{:S(2)}) collective-permute-start(bf16[32,768]{1,0:T(8,128)(2,1)S(1)} %get-tuple-element.41), channel_id=1, source_target_pairs={{0,4},{1,5},{2,6},{3,7},{4,0},{5,1},{6,2},{7,3},{8,12},{9,13},{10,... | collective-permute-start | bytes 147464 | tf_op jit(solution)/shard_map/ppermute | solution.py:78
  45.1 4.1 %collective-permute-start.9 = (bf16[32,768]{1,0:T(8,128)(2,1)S(1)}, bf16[32,768]{1,0:T(8,128)(2,1)S(1)}, u32[]{:S(2)}, u32[]{:S(2)}) collective-permute-start(bf16[32,768]{1,0:T(8,128)(2,1)S(1)} %get-tuple-element.42), channel_id=1, source_target_pairs={{0,2},{1,3},{2,0},{3,1},{4,6},{5,7},{6,4},{7,5},{8,10},{9,11},{10,... | collective-permute-start | bytes 147464 | tf_op jit(solution)/shard_map/ppermute | solution.py:78

commit v5 on v4

--- a/solution.py
+++ b/solution.py
@@ -173,8 +173,8 @@
 
 
 FETCH_COST = pl.CostEstimate(flops=5_000_000_000, bytes_accessed=0, transcendentals=0)
-SCOPE = 18 * MIB
-SLOTS = 4
+SCOPE = 16 * MIB
+SLOTS = 3
 CUT = 512
 SUB = 512
 
@@ -199,13 +199,17 @@
     )(wu)
 
 
-def near_body(own, mate, expo, wg, up_near, wu, acc_g, acc_u, limits, up_far, left, sem):
+def near_body(
+    own, mate, expo, wg, up_near, wu, wd, acc_g, acc_u, limits, up_far, down_first, left, sem
+):
     chip, core = place()
     rows = own.shape[0]
     width = own.shape[1] - LANES
     depth = 2 * width
+    slab = wd.at[0, pl.ds(0, down_first.shape[0])]
+    copies = [pltpu.make_async_copy(slab, down_first, sem.at[up_near.shape[1] // TILE])]
+    copies[0].start()
     fill_left(left, own, mate, core, width)
-    copies = []
     for index in range(up_near.shape[1] // TILE):
         columns = slice(index * TILE, (index + 1) * TILE)
         acc_u[:, columns] = jnp.dot(left[...], up_near[:, columns], preferred_element_type=F32)
@@ -233,30 +237,37 @@
         copy.wait()
 
 
-def near(own, mate, expo, wg, up_near, wu):
+def near(own, mate, expo, wg, up_near, wu, wd):
     rows = own.shape[0]
     depth, units = up_near.shape
     acc = pltpu.VMEM((rows, units), F32)
     return pl.pallas_call(
         near_body,
-        in_specs=[VMEM] * 5 + [HBM],
-        out_specs=[VMEM] * 4,
-        out_shape=[acc, acc, pltpu.VMEM((rows, expo.shape[0]), F32), pltpu.VMEM((depth, units), BF16)],
+        in_specs=[VMEM] * 5 + [HBM] * 2,
+        out_specs=[VMEM] * 5,
+        out_shape=[
+            acc,
+            acc,
+            pltpu.VMEM((rows, expo.shape[0]), F32),
+            pltpu.VMEM((depth, units), BF16),
+            pltpu.VMEM((CUT, wd.shape[2]), BF16),
+        ],
         input_output_aliases={4: 3},
         scratch_shapes=[
             pltpu.VMEM((rows, depth), BF16),
-            pltpu.SemaphoreType.DMA((units // TILE,)),
+            pltpu.SemaphoreType.DMA((units // TILE + 1,)),
         ],
         cost_estimate=pl.CostEstimate(
             flops=4 * rows * depth * units, bytes_accessed=2 * depth * units, transcendentals=0
         ),
         compiler_params=pltpu.CompilerParams(vmem_limit_bytes=SCOPE),
         name="near",
-    )(own, mate, expo, wg, up_near, wu)
+    )(own, mate, expo, wg, up_near, wu, wd)
 
 
 def far_body(
-    own, mate, cross, cross_mate, expo, acc_g, acc_u, limits, up_far, wg, wd, send, keep,
+    own, mate, cross, cross_mate, expo, acc_g, acc_u, limits, up_far, down_first, wg, wd,
+    send, keep,
     left, partial, buf, sem,
 ):
     del expo
@@ -272,7 +283,7 @@
         part = wd.at[0, pl.ds(unit * CUT, CUT)]
         return pltpu.make_async_copy(part, buf.at[unit % slots], sem.at[unit % slots])
 
-    for unit in range(slots):
+    for unit in range(1, slots + 1):
         copy(unit).start()
     fill_left(left, cross, cross_mate, core, width)
 
@@ -304,10 +315,12 @@
             )
             pieces.append((gate / (1.0 + jnp.exp(-gate)) * up).astype(BF16))
         hidden = jnp.concatenate(pieces, axis=1)
-        copy(unit).wait()
-        term = jnp.dot(hidden, buf[unit % slots], preferred_element_type=F32)
+        if unit > 0:
+            copy(unit).wait()
+        slab = buf[unit % slots] if unit > 0 else down_first[...]
+        term = jnp.dot(hidden, slab, preferred_element_type=F32)
         partial[...] = term if unit == 0 else partial[...] + term
-        if unit + slots < cuts:
+        if 0 < unit < cuts - slots:
             copy(unit + slots).start()
 
     blocks = lax.broadcasted_iota(jnp.int32, limits.shape, 1)
@@ -324,13 +337,13 @@
             out[block % 2, :, columns] = (coded * weight).astype(out.dtype)
 
 
-def far(own, mate, cross, cross_mate, expo, acc_g, acc_u, limits, up_far, wg, wd):
+def far(own, mate, cross, cross_mate, expo, acc_g, acc_u, limits, up_far, down_first, wg, wd):
     rows = own.shape[0]
     depth, units = up_far.shape
     width = depth // 2
     return pl.pallas_call(
         far_body,
-        in_specs=[VMEM] * 10 + [HBM],
+        in_specs=[VMEM] * 11 + [HBM],
         out_specs=[VMEM, VMEM],
         out_shape=[pltpu.VMEM((2, rows, width), BF16), pltpu.VMEM((2, rows, width), F32)],
         scratch_shapes=[
@@ -344,7 +357,7 @@
         ),
         compiler_params=pltpu.CompilerParams(vmem_limit_bytes=SCOPE),
         name="far",
-    )(own, mate, cross, cross_mate, expo, acc_g, acc_u, limits, up_far, wg, wd)
+    )(own, mate, cross, cross_mate, expo, acc_g, acc_u, limits, up_far, down_first, wg, wd)
 
 
 def split_body(keep, got, *outs):
@@ -391,7 +404,7 @@
 
 def fast(tokens, router_weight, routes, slots, gate_weight, up_weight, down_weight, scale_exponents):
     packed = pack(tokens, router_weight.T, routes.T, slots.T)
-    up_weight = in_hbm(up_weight)
+    up_weight, down_weight = in_hbm(up_weight), in_hbm(down_weight)
     wg = in_vmem(gate_weight[0])
     arrived = [swap(packed, bits, 0) for bits in (1, 2, 3)]
     packed, up_near = lax.optimization_barrier((packed, fetch(up_weight)))
@@ -399,12 +412,12 @@
     mate = in_vmem(swap(own, 0, 1))
     cross = swap(own, 0, 2)
     expo = in_vmem(scale_exponents[0, 0].T)
-    held = near(own, mate, expo, wg, in_vmem(up_near), up_weight)
+    held = near(own, mate, expo, wg, in_vmem(up_near), up_weight, down_weight)
     cross, *held = lax.optimization_barrier((cross, *held))
     cross = in_vmem(cross)
     cross_mate = in_vmem(swap(cross, 0, 1))
     send, keep = far(
-        own, mate, cross, cross_mate, expo, *map(in_vmem, held), wg, in_hbm(down_weight)
+        own, mate, cross, cross_mate, expo, *map(in_vmem, held), wg, down_weight
     )
     blocks = split(in_vmem(keep), in_vmem(swap(send, 0, 1)))
     parts = [blocks[0]]

time: 50 us -> 50.2 us (level)
  Pallas kernels: 22.2 us -> 23.2 us
  waiting for transfers between devices: 8.66 us -> 7.98 us
    pallas_call x2, Pallas kernels: 15.3 us -> 16.2 us  [the longest x1 10.3 us: far(): pl.pallas_call(far_body, in_specs=[VMEM] * 11 + [HBM], out_specs=[VMEM, V...]
    ppermute x14, waiting for transfers between devices: 8.66 us -> 7.98 us  [swap(): return lax.ppermute(value, JOINT, pairs)]
  transfers between devices with their start and end apart: 14 -> 14, of which waited for: 9 -> 9; matrix products, arithmetic and copies ran while one was open for 0% -> 0% of each run, Pallas kernels for 21% -> 22%
where the time goes in v5:
time: 50.2 us; the launch traced here: 50.1 us
  Pallas kernels  23.2 us (46%)
  starting transfers between devices  18.7 us (37%)
  waiting for transfers between devices  7.98 us (16%)
    ppermute x14, starting transfers between devices, swap(): return lax.ppermute(value, JOINT, pairs)  18.7 us
    pallas_call x1, Pallas kernels, far(): pl.pallas_call(far_body, in_specs=[VMEM] * 11 + [HBM], out_specs=[VMEM, V...  10.3 us
    ppermute x14, waiting for transfers between devices, swap(): return lax.ppermute(value, JOINT, pairs)  7.98 us
    pallas_call x1, Pallas kernels, near(): pl.pallas_call(near_body, in_specs=[VMEM] * 5 + [HBM] * 2, out_specs=[VME...  5.95 us
    pallas_call x1, Pallas kernels, fetch(): pl.pallas_call(fetch_body, in_specs=[HBM], out_specs=VMEM, out_shape=pltp...  5.04 us
    pallas_call x1, Pallas kernels, pack(): pl.pallas_call(pack_body, in_specs=[HBM] * 4, out_specs=VMEM, out_shape=p...  1.11 us
  transfers between devices with their start and end apart: 14, of which 9 were waited for; matrix products, arithmetic and copies ran while one was open for 0% of the time, Pallas kernels for 22%

profile of v5, /device:TPU:0, one launch (start us, length us, event | category | flops | bytes accessed | tf_op | source)
XLA Modules:
  0.0 50.1 jit_solution(13148607019286117101)
XLA Ops:
  0.0 1.1 %pack.1.refs_0_ = bf16[32,896]{1,0:T(8,128)(2,1)S(1)} custom-call(bf16[32,768]{1,0:T(8,128)(2,1)} %tokens.1, f32[4,768]{1,0:T(4,128)} %bitcast.13, s32[2,32]{1,0:T(2,128)} %bitcast.14, s32[2,32]{1,0:T(2,128)} %bitcast.15), custom_call_target="tpu_custom_call" | custom-call | flops 12000000000 | tf_op jit(solution)/shard_map/pack/pallas_call | solution.py:126
  1.2 3.1 %collective-permute-start = (bf16[32,896]{1,0:T(8,128)(2,1)S(1)}, bf16[32,896]{1,0:T(8,128)(2,1)S(1)}, u32[]{:S(2)}, u32[]{:S(2)}) collective-permute-start(bf16[32,896]{1,0:T(8,128)(2,1)S(1)} %pack.1.refs_0_), channel_id=1, source_target_pairs={{0,4},{1,5},{2,6},{3,7},{4,0},{5,1},{6,2},{7,3},{8,12},{9,13},{10,... | collective-permute-start | bytes 172040 | tf_op jit(solution)/shard_map/ppermute | solution.py:78
  4.3 2.6 %collective-permute-start.1 = (bf16[32,896]{1,0:T(8,128)(2,1)S(1)}, bf16[32,896]{1,0:T(8,128)(2,1)S(1)}, u32[]{:S(2)}, u32[]{:S(2)}) collective-permute-start(bf16[32,896]{1,0:T(8,128)(2,1)S(1)} %pack.1.refs_0_), channel_id=1, source_target_pairs={{0,8},{1,9},{2,10},{3,11},{4,12},{5,13},{6,14},{7,15},{8,0},{9,1},... | collective-permute-start | bytes 172040 | tf_op jit(solution)/shard_map/ppermute | solution.py:78
  6.9 5.0 %fetch.1.up_near = bf16[1536,4096]{1,0:T(8,128)(2,1)S(1)} custom-call(bf16[1,3072,4096]{2,1,0:T(8,128)(2,1)} %wu.3), custom_call_target="tpu_custom_call" | custom-call | flops 5000000000 | tf_op jit(solution)/shard_map/fetch/pallas_call | solution.py:190
  11.9 0.9 %collective-permute-done.2.refs_3_ = bf16[32,896]{1,0:T(8,128)(2,1)S(1)} collective-permute-done((bf16[32,896]{1,0:T(8,128)(2,1)S(1)}, bf16[32,896]{1,0:T(8,128)(2,1)S(1)}, u32[]{:S(2)}, u32[]{:S(2)}) %collective-permute-start.2) | collective-permute-done | bytes 57376 | tf_op jit(solution)/shard_map/ppermute | solution.py:78
  12.9 1.6 %collective-permute-start.4 = (bf16[128,896]{1,0:T(8,128)(2,1)S(1)}, bf16[128,896]{1,0:T(8,128)(2,1)S(1)}, u32[]{:S(2)}, u32[]{:S(2)}) collective-permute-start(bf16[128,896]{1,0:T(8,128)(2,1)S(1)} %join.1.own), channel_id=1, source_target_pairs={{0,2},{1,3},{2,0},{3,1},{4,6},{5,7},{6,4},{7,5},{8,10},{9,11},{10,... | collective-permute-start | bytes 688136 | tf_op jit(solution)/shard_map/ppermute | solution.py:78
  14.6 5.9 %near.1 = (f32[128,4096]{1,0:T(8,128)S(1)}, f32[128,4096]{1,0:T(8,128)S(1)}, f32[128,24]{1,0:T(8,128)S(1)}, bf16[1536,4096]{1,0:T(8,128)(2,1)S(1)}, bf16[512,3072]{1,0:T(8,128)(2,1)S(1)}) custom-call(bf16[128,896]{1,0:T(8,128)(2,1)S(1)} %join.1.own, bf16[128,896]{1,0:T(8,128)(2,1)S(1)} %collective-permute-done.3.mate, ...), custom_call_target="tpu_custom_call", output_to_operand_aliasing={{3}: (4, {})} | custom-call | flops 3221225472 | bytes 12582912 | tf_op jit(solution)/shard_map/near/pallas_call | solution.py:244
  20.5 0.4 collective-permute-done.4.cross
  21.0 1.5 %collective-permute-done.5.cross_mate = bf16[128,896]{1,0:T(8,128)(2,1)S(1)} collective-permute-done((bf16[128,896]{1,0:T(8,128)(2,1)S(1)}, bf16[128,896]{1,0:T(8,128)(2,1)S(1)}, u32[]{:S(2)}, u32[]{:S(2)}) %collective-permute-start.5) | collective-permute-done | bytes 229408 | tf_op jit(solution)/shard_map/ppermute | solution.py:78
  22.4 10.3 %far.1 = (bf16[2,128,768]{2,1,0:T(8,128)(2,1)S(1)}, f32[2,128,768]{2,1,0:T(8,128)S(1)}) custom-call(bf16[128,896]{1,0:T(8,128)(2,1)S(1)} %join.1.own, bf16[128,896]{1,0:T(8,128)(2,1)S(1)} %collective-permute-done.3.mate, bf16[128,896]{1,0:T(8,128)(2,1)S(1)} %collective-permute-done.4.cross, bf16[128,896]{1,0:T(8,128)(2,1)S(1)} %collective-permute-done.5.cross_mate, ...), custom_call_target="tpu_custom_call" | custom-call | flops 6442450944 | bytes 25165824 | tf_op jit(solution)/shard_map/far/pallas_call | solution.py:344
  32.7 0.2 collective-permute-start.6
  32.9 1.6 %collective-permute-done.6.got = bf16[2,128,768]{2,1,0:T(8,128)(2,1)S(1)} collective-permute-done((bf16[2,128,768]{2,1,0:T(8,128)(2,1)S(1)}, bf16[2,128,768]{2,1,0:T(8,128)(2,1)S(1)}, u32[]{:S(2)}, u32[]{:S(2)}) %collective-permute-start.6) | collective-permute-done | bytes 393248 | tf_op jit(solution)/shard_map/ppermute | solution.py:78
  34.6 4.3 %collective-permute-start.10 = (bf16[32,768]{1,0:T(8,128)(2,1)S(1)}, bf16[32,768]{1,0:T(8,128)(2,1)S(1)}, u32[]{:S(2)}, u32[]{:S(2)}) collective-permute-start(bf16[32,768]{1,0:T(8,128)(2,1)S(1)} %get-tuple-element.47), channel_id=1, source_target_pairs={{0,14},{1,15},{2,12},{3,13},{4,10},{5,11},{6,8},{7,9},{8,6},{9,7},... | collective-permute-start | bytes 147464 | tf_op jit(solution)/shard_map/ppermute | solution.py:78
  38.9 0.5 %collective-permute-start.11 = (bf16[32,768]{1,0:T(8,128)(2,1)S(1)}, bf16[32,768]{1,0:T(8,128)(2,1)S(1)}, u32[]{:S(2)}, u32[]{:S(2)}) collective-permute-start(bf16[32,768]{1,0:T(8,128)(2,1)S(1)} %get-tuple-element.48), channel_id=1, source_target_pairs={{0,12},{1,13},{2,14},{3,15},{4,8},{5,9},{6,10},{7,11},{8,4},{9,5},... | collective-permute-start | bytes 147464 | tf_op jit(solution)/shard_map/ppermute | solution.py:78
  39.5 2.9 %collective-permute-start.13 = (bf16[32,768]{1,0:T(8,128)(2,1)S(1)}, bf16[32,768]{1,0:T(8,128)(2,1)S(1)}, u32[]{:S(2)}, u32[]{:S(2)}) collective-permute-start(bf16[32,768]{1,0:T(8,128)(2,1)S(1)} %get-tuple-element.50), channel_id=1, source_target_pairs={{0,8},{1,9},{2,10},{3,11},{4,12},{5,13},{6,14},{7,15},{8,0},{9,1},... | collective-permute-start | bytes 147464 | tf_op jit(solution)/shard_map/ppermute | solution.py:78
  42.3 1.9 %collective-permute-start.7 = (bf16[32,768]{1,0:T(8,128)(2,1)S(1)}, bf16[32,768]{1,0:T(8,128)(2,1)S(1)}, u32[]{:S(2)}, u32[]{:S(2)}) collective-permute-start(bf16[32,768]{1,0:T(8,128)(2,1)S(1)} %get-tuple-element.44), channel_id=1, source_target_pairs={{0,6},{1,7},{2,4},{3,5},{4,2},{5,3},{6,0},{7,1},{8,14},{9,15},{10,... | collective-permute-start | bytes 147464 | tf_op jit(solution)/shard_map/ppermute | solution.py:78
  44.2 1.1 %collective-permute-start.8 = (bf16[32,768]{1,0:T(8,128)(2,1)S(1)}, bf16[32,768]{1,0:T(8,128)(2,1)S(1)}, u32[]{:S(2)}, u32[]{:S(2)}) collective-permute-start(bf16[32,768]{1,0:T(8,128)(2,1)S(1)} %get-tuple-element.45), channel_id=1, source_target_pairs={{0,4},{1,5},{2,6},{3,7},{4,0},{5,1},{6,2},{7,3},{8,12},{9,13},{10,... | collective-permute-start | bytes 147464 | tf_op jit(solution)/shard_map/ppermute | solution.py:78
  45.3 0.5 %collective-permute-start.9 = (bf16[32,768]{1,0:T(8,128)(2,1)S(1)}, bf16[32,768]{1,0:T(8,128)(2,1)S(1)}, u32[]{:S(2)}, u32[]{:S(2)}) collective-permute-start(bf16[32,768]{1,0:T(8,128)(2,1)S(1)} %get-tuple-element.46), channel_id=1, source_target_pairs={{0,2},{1,3},{2,0},{3,1},{4,6},{5,7},{6,4},{7,5},{8,10},{9,11},{10,... | collective-permute-start | bytes 147464 | tf_op jit(solution)/shard_map/ppermute | solution.py:78
  45.8 0.7 %collective-permute-done.12.refs_6_ = bf16[32,768]{1,0:T(8,128)(2,1)S(1)} collective-permute-done((bf16[32,768]{1,0:T(8,128)(2,1)S(1)}, bf16[32,768]{1,0:T(8,128)(2,1)S(1)}, u32[]{:S(2)}, u32[]{:S(2)}) %collective-permute-start.12) | collective-permute-done | bytes 49184 | tf_op jit(solution)/shard_map/ppermute | solution.py:78
  46.5 0.8 %collective-permute-done.13.refs_7_ = bf16[32,768]{1,0:T(8,128)(2,1)S(1)} collective-permute-done((bf16[32,768]{1,0:T(8,128)(2,1)S(1)}, bf16[32,768]{1,0:T(8,128)(2,1)S(1)}, u32[]{:S(2)}, u32[]{:S(2)}) %collective-permute-start.13) | collective-permute-done | bytes 49184 | tf_op jit(solution)/shard_map/ppermute | solution.py:78
  47.3 1.1 %collective-permute-done.7.refs_1_ = bf16[32,768]{1,0:T(8,128)(2,1)S(1)} collective-permute-done((bf16[32,768]{1,0:T(8,128)(2,1)S(1)}, bf16[32,768]{1,0:T(8,128)(2,1)S(1)}, u32[]{:S(2)}, u32[]{:S(2)}) %collective-permute-start.7) | collective-permute-done | bytes 49184 | tf_op jit(solution)/shard_map/ppermute | solution.py:78
  48.4 0.1 collective-permute-done.8.refs_2_
  48.6 0.8 %collective-permute-done.9.refs_3_ = bf16[32,768]{1,0:T(8,128)(2,1)S(1)} collective-permute-done((bf16[32,768]{1,0:T(8,128)(2,1)S(1)}, bf16[32,768]{1,0:T(8,128)(2,1)S(1)}, u32[]{:S(2)}, u32[]{:S(2)}) %collective-permute-start.9) | collective-permute-done | bytes 49184 | tf_op jit(solution)/shard_map/ppermute | solution.py:78
  49.4 0.7 %total.1 = bf16[32,768]{1,0:T(8,128)(2,1)} custom-call(f32[32,768]{1,0:T(8,128)S(1)} %get-tuple-element.43.refs_0_, bf16[32,768]{1,0:T(8,128)(2,1)S(1)} %collective-permute-done.7.refs_1_, bf16[32,768]{1,0:T(8,128)(2,1)S(1)} %collective-permute-done.8.refs_2_, bf16[32,768]{1,0:T(8,128)(2,1)S(1)} %collective-permute-done.9.refs_3_, ...), custom_call_target="tpu_custom_call" | custom-call | tf_op jit(solution)/shard_map/total/pallas_call | solution.py:392
  (26 shorter events, 0.2 us)
Async XLA Ops:
  0.0 14.5 %slice-start = ((s8[25165824]{0:T(1024)(128)(4,1)}), s8[4194304]{0:T(1024)(128)(4,1)S(1)}, s32[]{:S(2)}) async-start(s8[25165824]{0:T(1024)(128)(4,1)} %bitcast.7), calls=%async_computation | async-start | bytes 8388608
  0.0 14.5 %slice-start.1 = ((s8[25165824]{0:T(1024)(128)(4,1)}), s8[4194304]{0:T(1024)(128)(4,1)S(1)}, s32[]{:S(2)}) async-start(s8[25165824]{0:T(1024)(128)(4,1)} %bitcast.7), calls=%async_computation.1 | async-start | bytes 8388608
  0.0 14.5 %slice-start.2 = ((s8[25165824]{0:T(1024)(128)(4,1)}), s8[4194304]{0:T(1024)(128)(4,1)S(1)}, s32[]{:S(2)}) async-start(s8[25165824]{0:T(1024)(128)(4,1)} %bitcast.7), calls=%async_computation.2 | async-start | bytes 8388608
  0.0 14.5 %slice-start.3 = ((s8[25165824]{0:T(1024)(128)(4,1)}), s8[4194304]{0:T(1024)(128)(4,1)S(1)}, s32[]{:S(2)}) async-start(s8[25165824]{0:T(1024)(128)(4,1)} %bitcast.7), calls=%async_computation.3 | async-start | bytes 8388608
  1.1 13.4 %slice-start.4 = ((s8[25165824]{0:T(1024)(128)(4,1)}), s8[4194304]{0:T(1024)(128)(4,1)S(1)}, s32[]{:S(2)}) async-start(s8[25165824]{0:T(1024)(128)(4,1)} %bitcast.7), calls=%async_computation.4 | async-start | bytes 8388608
  1.1 13.4 %slice-start.5 = ((s8[25165824]{0:T(1024)(128)(4,1)}), s8[4194304]{0:T(1024)(128)(4,1)S(1)}, s32[]{:S(2)}) async-start(s8[25165824]{0:T(1024)(128)(4,1)} %bitcast.7), calls=%async_computation.5 | async-start | bytes 8388608
  1.2 13.4 %copy-start = (s32[1,1,128,24]{2,3,1,0:T(8,128)S(1)}, s32[1,1,128,24]{2,3,1,0:T(8,128)}, u32[]{:S(2)}) copy-start(s32[1,1,128,24]{2,3,1,0:T(8,128)} %param.15) | copy-start | bytes 36868
  1.2 10.7 %collective-permute-start = (bf16[32,896]{1,0:T(8,128)(2,1)S(1)}, bf16[32,896]{1,0:T(8,128)(2,1)S(1)}, u32[]{:S(2)}, u32[]{:S(2)}) collective-permute-start(bf16[32,896]{1,0:T(8,128)(2,1)S(1)} %pack.1.refs_0_), channel_id=1, source_target_pairs={{0,4},{1,5},{2,6},{3,7},{4,0},{5,1},{6,2},{7,3},{8,12},{9,13},{10,... | collective-permute-start | bytes 172040 | tf_op jit(solution)/shard_map/ppermute | solution.py:78
  4.3 7.6 %collective-permute-start.1 = (bf16[32,896]{1,0:T(8,128)(2,1)S(1)}, bf16[32,896]{1,0:T(8,128)(2,1)S(1)}, u32[]{:S(2)}, u32[]{:S(2)}) collective-permute-start(bf16[32,896]{1,0:T(8,128)(2,1)S(1)} %pack.1.refs_0_), channel_id=1, source_target_pairs={{0,8},{1,9},{2,10},{3,11},{4,12},{5,13},{6,14},{7,15},{8,0},{9,1},... | collective-permute-start | bytes 172040 | tf_op jit(solution)/shard_map/ppermute | solution.py:78
  6.9 6.0 %collective-permute-start.2 = (bf16[32,896]{1,0:T(8,128)(2,1)S(1)}, bf16[32,896]{1,0:T(8,128)(2,1)S(1)}, u32[]{:S(2)}, u32[]{:S(2)}) collective-permute-start(bf16[32,896]{1,0:T(8,128)(2,1)S(1)} %pack.1.refs_0_), channel_id=1, source_target_pairs={{0,12},{1,13},{2,14},{3,15},{4,8},{5,9},{6,10},{7,11},{8,4},{9,5},... | collective-permute-start | bytes 172040 | tf_op jit(solution)/shard_map/ppermute | solution.py:78
  12.9 1.6 %collective-permute-start.3 = (bf16[128,896]{1,0:T(8,128)(2,1)S(1)}, bf16[128,896]{1,0:T(8,128)(2,1)S(1)}, u32[]{:S(2)}, u32[]{:S(2)}) collective-permute-start(bf16[128,896]{1,0:T(8,128)(2,1)S(1)} %join.1.own), channel_id=1, source_target_pairs={{0,1},{1,0},{2,3},{3,2},{4,5},{5,4},{6,7},{7,6},{8,9},{9,8},{10,11... | collective-permute-start | bytes 688136 | tf_op jit(solution)/shard_map/ppermute | solution.py:78
  12.9 8.0 %collective-permute-start.4 = (bf16[128,896]{1,0:T(8,128)(2,1)S(1)}, bf16[128,896]{1,0:T(8,128)(2,1)S(1)}, u32[]{:S(2)}, u32[]{:S(2)}) collective-permute-start(bf16[128,896]{1,0:T(8,128)(2,1)S(1)} %join.1.own), channel_id=1, source_target_pairs={{0,2},{1,3},{2,0},{3,1},{4,6},{5,7},{6,4},{7,5},{8,10},{9,11},{10,... | collective-permute-start | bytes 688136 | tf_op jit(solution)/shard_map/ppermute | solution.py:78
  21.0 1.5 %collective-permute-start.5 = (bf16[128,896]{1,0:T(8,128)(2,1)S(1)}, bf16[128,896]{1,0:T(8,128)(2,1)S(1)}, u32[]{:S(2)}, u32[]{:S(2)}) collective-permute-start(bf16[128,896]{1,0:T(8,128)(2,1)S(1)} %collective-permute-done.4.cross), channel_id=1, source_target_pairs={{0,1},{1,0},{2,3},{3,2},{4,5},{5,4},{6,7},{7,6},{8,9},{9,8},{10,11... | collective-permute-start | bytes 688136 | tf_op jit(solution)/shard_map/ppermute | solution.py:78
  32.7 1.8 %collective-permute-start.6 = (bf16[2,128,768]{2,1,0:T(8,128)(2,1)S(1)}, bf16[2,128,768]{2,1,0:T(8,128)(2,1)S(1)}, u32[]{:S(2)}, u32[]{:S(2)}) collective-permute-start(bf16[2,128,768]{2,1,0:T(8,128)(2,1)S(1)} %get-tuple-element.42), channel_id=1, source_target_pairs={{0,1},{1,0},{2,3},{3,2},{4,5},{5,4},{6,7},{7,6},{8,9},{9,8},{10,11... | collective-permute-start | bytes 1179656 | tf_op jit(solution)/shard_map/ppermute | solution.py:78
  34.6 9.6 %collective-permute-start.10 = (bf16[32,768]{1,0:T(8,128)(2,1)S(1)}, bf16[32,768]{1,0:T(8,128)(2,1)S(1)}, u32[]{:S(2)}, u32[]{:S(2)}) collective-permute-start(bf16[32,768]{1,0:T(8,128)(2,1)S(1)} %get-tuple-element.47), channel_id=1, source_target_pairs={{0,14},{1,15},{2,12},{3,13},{4,10},{5,11},{6,8},{7,9},{8,6},{9,7},... | collective-permute-start | bytes 147464 | tf_op jit(solution)/shard_map/ppermute | solution.py:78
  38.9 6.4 %collective-permute-start.11 = (bf16[32,768]{1,0:T(8,128)(2,1)S(1)}, bf16[32,768]{1,0:T(8,128)(2,1)S(1)}, u32[]{:S(2)}, u32[]{:S(2)}) collective-permute-start(bf16[32,768]{1,0:T(8,128)(2,1)S(1)} %get-tuple-element.48), channel_id=1, source_target_pairs={{0,12},{1,13},{2,14},{3,15},{4,8},{5,9},{6,10},{7,11},{8,4},{9,5},... | collective-permute-start | bytes 147464 | tf_op jit(solution)/shard_map/ppermute | solution.py:78
  39.4 7.0 %collective-permute-start.12 = (bf16[32,768]{1,0:T(8,128)(2,1)S(1)}, bf16[32,768]{1,0:T(8,128)(2,1)S(1)}, u32[]{:S(2)}, u32[]{:S(2)}) collective-permute-start(bf16[32,768]{1,0:T(8,128)(2,1)S(1)} %get-tuple-element.49), channel_id=1, source_target_pairs={{0,10},{1,11},{2,8},{3,9},{4,14},{5,15},{6,12},{7,13},{8,2},{9,3},... | collective-permute-start | bytes 147464 | tf_op jit(solution)/shard_map/ppermute | solution.py:78
  39.5 7.9 %collective-permute-start.13 = (bf16[32,768]{1,0:T(8,128)(2,1)S(1)}, bf16[32,768]{1,0:T(8,128)(2,1)S(1)}, u32[]{:S(2)}, u32[]{:S(2)}) collective-permute-start(bf16[32,768]{1,0:T(8,128)(2,1)S(1)} %get-tuple-element.50), channel_id=1, source_target_pairs={{0,8},{1,9},{2,10},{3,11},{4,12},{5,13},{6,14},{7,15},{8,0},{9,1},... | collective-permute-start | bytes 147464 | tf_op jit(solution)/shard_map/ppermute | solution.py:78
  42.3 6.1 %collective-permute-start.7 = (bf16[32,768]{1,0:T(8,128)(2,1)S(1)}, bf16[32,768]{1,0:T(8,128)(2,1)S(1)}, u32[]{:S(2)}, u32[]{:S(2)}) collective-permute-start(bf16[32,768]{1,0:T(8,128)(2,1)S(1)} %get-tuple-element.44), channel_id=1, source_target_pairs={{0,6},{1,7},{2,4},{3,5},{4,2},{5,3},{6,0},{7,1},{8,14},{9,15},{10,... | collective-permute-start | bytes 147464 | tf_op jit(solution)/shard_map/ppermute | solution.py:78
  44.2 4.4 %collective-permute-start.8 = (bf16[32,768]{1,0:T(8,128)(2,1)S(1)}, bf16[32,768]{1,0:T(8,128)(2,1)S(1)}, u32[]{:S(2)}, u32[]{:S(2)}) collective-permute-start(bf16[32,768]{1,0:T(8,128)(2,1)S(1)} %get-tuple-element.45), channel_id=1, source_target_pairs={{0,4},{1,5},{2,6},{3,7},{4,0},{5,1},{6,2},{7,3},{8,12},{9,13},{10,... | collective-permute-start | bytes 147464 | tf_op jit(solution)/shard_map/ppermute | solution.py:78
  45.3 4.1 %collective-permute-start.9 = (bf16[32,768]{1,0:T(8,128)(2,1)S(1)}, bf16[32,768]{1,0:T(8,128)(2,1)S(1)}, u32[]{:S(2)}, u32[]{:S(2)}) collective-permute-start(bf16[32,768]{1,0:T(8,128)(2,1)S(1)} %get-tuple-element.46), channel_id=1, source_target_pairs={{0,2},{1,3},{2,0},{3,1},{4,6},{5,7},{6,4},{7,5},{8,10},{9,11},{10,... | collective-permute-start | bytes 147464 | tf_op jit(solution)/shard_map/ppermute | solution.py:78
